TPU v7x, 32 devices: a whole 2x2x4 slice. The times are simulated.
32 devices in a mesh: row: 4 (over y, x), seq: 8 (over z, core).
Axes of the slice: x: 2, y: 2, z: 4, core: 2. Of those that a mesh axis runs over, the one named last changes fastest.
Arguments:
- mixer_input: bfloat16 [8192, 4352], P(('row', 'seq')), parts along dimension 0, may hold values from -6 to 6
- gate_input: bfloat16 [8192, 4096], P(('row', 'seq')), parts along dimension 0, may hold values from -6 to 6
- conv_forward: float32 [4, 4352], replicated, may hold values from -3 to 3
- conv_reverse: float32 [4, 4352], replicated, may hold values from -3 to 3
- step_size: float32 [64, 8192], P(None, ('row', 'seq')), parts along dimension 1, may hold values from 0 to 1, as said below
- decay_rate: float32 [256], P('row'), parts along dimension 0, may hold values from 1 to 8, as said below
- skip_scale: float32 [64], replicated, may hold values from 0.5 to 1.5
- norm_gain: float32 [4096], replicated, may hold values from 0.5 to 1.5
Outputs:
- mixer_output: bfloat16 [8192, 4096], P(('row', 'seq')), parts along dimension 0
There are 4 independent parts, one for each index of `row`. A program takes and returns all parts, laid end to end along the dimension named above; an argument that names none is the same for every part. Nothing has to cross between parts.
Inputs may be any that keep to these rules, and one draw needn't show every extreme that they name: `step_size`: positive step sizes. `decay_rate`: positive coefficients.
All inputs are finite; a program needn't handle non-finite values.
Results may differ from a plain program's by a relative error of at most 0.007.
Values may be sent and summed in bfloat16 or wider, within the bound.
A program may use at most 192 MiB of HBM per device.

v0:
```python
import jax
import jax.numpy as jnp
from jax import lax
from jax.sharding import PartitionSpec as P

HEADS = 64
HEAD_DIM = 64
STATE = 128
WIDTH = 4
GROUP = 256


def with_halo(cells, sides, width):
    for axis, dim in sides:
        count = lax.axis_size(axis)
        ends = count - 1
        head = lax.slice_in_dim(cells, 0, width, axis=dim)
        tail = lax.slice_in_dim(cells, cells.shape[dim] - width, cells.shape[dim], axis=dim)
        cells = jnp.concatenate(
            [
                lax.ppermute(tail, axis, [(i, (i + 1) % count) for i in range(ends)]),
                cells,
                lax.ppermute(head, axis, [((i + 1) % count, i) for i in range(ends)]),
            ],
            axis=dim,
        )
    return cells


def entering(array, axis, combine, identity, reverse):
    devices, mine = (lax.axis_size(axis), lax.axis_index(axis))
    everything = jax.tree.map(lambda part: lax.all_gather(part, axis), array)
    start = jax.tree.map(
        lambda part, zero: jnp.broadcast_to(jnp.asarray(zero, part.dtype), part.shape),
        array,
        identity,
    )

    def lap(k, before):
        at = devices - 1 - k if reverse else k
        reached = at > mine if reverse else at < mine
        new = combine(before, jax.tree.map(lambda part: part[at], everything))
        return jax.tree.map(lambda a, b: jnp.where(reached, a, b), new, before)

    return lax.fori_loop(0, devices, lap, start)


def conv_pair(padded, conv_forward, conv_reverse, length):
    reach = conv_forward.shape[0] - 1
    ahead = jnp.zeros((length, padded.shape[1]), jnp.float32)
    behind = jnp.zeros((length, padded.shape[1]), jnp.float32)
    for kernel_tap in range(reach + 1):
        ahead = ahead + conv_forward[kernel_tap] * padded[kernel_tap : kernel_tap + length]
        start = 2 * reach - kernel_tap
        behind = behind + conv_reverse[kernel_tap] * padded[start : start + length]
    return (jax.nn.silu(ahead).astype(jnp.bfloat16), jax.nn.silu(behind).astype(jnp.bfloat16))


def split_pieces(convolved):
    length = convolved.shape[0]
    inner = HEADS * HEAD_DIM
    values = convolved[:, :inner].reshape(length, HEADS, HEAD_DIM)
    keys = convolved[:, inner : inner + STATE]
    queries = convolved[:, inner + STATE :]
    return (values, keys, queries)


def block_terms(block_values, block_keys, block_queries, block_steps, decay_rate):
    log_steps = -decay_rate[:, None] * block_steps
    cumulative = jnp.cumsum(log_steps, axis=1)
    width = block_steps.shape[1]
    position = jnp.arange(width)
    causal = position[:, None] >= position[None, :]
    segment = jnp.where(causal[None], cumulative[:, :, None] - cumulative[:, None, :], -1e30)
    intersection = jnp.dot(block_queries, block_keys.T, preferred_element_type=jnp.float32)
    scores = (intersection[None] * jnp.exp(segment) * block_steps[:, None, :]).astype(jnp.bfloat16)
    within = jnp.einsum("hts,shp->thp", scores, block_values, preferred_element_type=jnp.float32)
    factors = block_steps * jnp.exp(cumulative[:, -1:] - cumulative)
    weighted = (block_values * factors.T[:, :, None]).astype(jnp.bfloat16)
    state = jnp.einsum("tn,thp->hpn", block_keys, weighted, preferred_element_type=jnp.float32)
    return (within, state, cumulative)


def local_pass(values, keys, queries, steps, decay_rate):
    block_count = values.shape[0] // GROUP
    value_blocks = values.reshape(block_count, GROUP, HEADS, HEAD_DIM)
    key_blocks = keys.reshape(block_count, GROUP, STATE)
    query_blocks = queries.reshape(block_count, GROUP, STATE)
    step_blocks = steps.reshape(HEADS, block_count, GROUP).transpose(1, 0, 2)
    within, states, cumulative = lax.map(
        lambda item: block_terms(item[0], item[1], item[2], item[3], decay_rate),
        (value_blocks, key_blocks, query_blocks, step_blocks),
    )
    ends = cumulative[:, :, -1]

    def advance(carry, item):
        return (jnp.exp(item[1])[:, None, None] * carry + item[0], carry)

    start_state = jnp.zeros((HEADS, HEAD_DIM, STATE), jnp.float32)
    total_state, entries = lax.scan(advance, start_state, (states, ends))
    offsets = jnp.cumsum(ends, axis=0) - ends
    total_decay = jnp.exp(jnp.sum(ends, axis=0))
    return (within, entries, cumulative, offsets, query_blocks, total_decay, total_state)


def finish(local_parts, carried):
    within, entries, cumulative, offsets, query_blocks = local_parts[:5]
    queries_wide = query_blocks.astype(jnp.float32)
    growth = jnp.exp(cumulative).transpose(0, 2, 1)[..., None]
    entries = entries + jnp.exp(offsets)[:, :, None, None] * carried[None]
    carried_term = jnp.einsum(
        "ctn,chpn->cthp", queries_wide, entries, precision=lax.Precision.HIGHEST
    )
    result = within + growth * carried_term
    return result.reshape(-1, HEADS, HEAD_DIM)


def combine(earlier, later):
    return (earlier[0] * later[0], later[0][:, None, None] * earlier[1] + later[1])


def per_device(
    mixer_input,
    gate_input,
    conv_forward,
    conv_reverse,
    step_size,
    decay_rate,
    skip_scale,
    norm_gain,
):
    length = mixer_input.shape[0]
    padded = with_halo(mixer_input, (("seq", 0),), WIDTH - 1)
    ahead, behind = conv_pair(padded, conv_forward, conv_reverse, length)
    values_ahead, keys_ahead, queries_ahead = split_pieces(ahead)
    values_behind, keys_behind, queries_behind = split_pieces(behind)
    forward_parts = local_pass(values_ahead, keys_ahead, queries_ahead, step_size, decay_rate)
    reverse_parts = local_pass(
        values_behind[::-1], keys_behind[::-1], queries_behind[::-1], step_size[:, ::-1], decay_rate
    )
    identity = (jnp.ones((HEADS,), jnp.float32), jnp.zeros((HEADS, HEAD_DIM, STATE), jnp.float32))
    forward_in = entering((forward_parts[5], forward_parts[6]), "seq", combine, identity, False)[1]
    reverse_in = entering((reverse_parts[5], reverse_parts[6]), "seq", combine, identity, True)[1]
    forward = finish(forward_parts, forward_in)
    reverse = finish(reverse_parts, reverse_in)[::-1]
    mixed = forward + reverse + skip_scale[None, :, None] * values_ahead
    gated = mixed.reshape(length, HEADS * HEAD_DIM) * jax.nn.silu(gate_input.astype(jnp.float32))
    scale = lax.rsqrt(jnp.mean(gated * gated, axis=-1, keepdims=True) + 1e-05)
    return (gated * scale * norm_gain).astype(jnp.bfloat16)


def solution(mesh):
    in_specs = (
        P(("row", "seq"), None),
        P(("row", "seq"), None),
        P(),
        P(),
        P(None, ("row", "seq")),
        P("row"),
        P(),
        P(),
    )
    out_specs = P(("row", "seq"), None)
    return jax.shard_map(
        per_device, mesh=mesh, in_specs=in_specs, out_specs=out_specs, check_vma=False
    )
```

profile of v0, /device:TPU:0, one launch (start us, length us, event | category | flops | bytes accessed | tf_op | source)
XLA Modules:
  0.0 389.3 jit_solution(17945366921073477110)
XLA Ops:
  8.9 3.0 collective-permute-start
  16.1 9.4 %multiply_convert_fusion.4 = (bf16[256,4352]{1,0:T(8,128)(2,1)S(1)}, bf16[256,4352]{1,0:T(8,128)(2,1)}) fusion(bf16[256,4352]{1,0:T(8,128)(2,1)} %param.12, bf16[259,4352]{1,0:T(8,128)(2,1)S(1)} %constant_dynamic-update-slice_fusion, f32[4352]{0:T(1024)S(1)} %get-tuple-element.355, f32[4352]{0:T(1024)S(1)} %get-tuple-element.356, ...), kind=kLoop, calls=%fused_computation.30 | loop fusion | flops 44564480 | bytes 13534720 | tf_op jit(solution)/shard_map/convert_element_type | solution.py:56
  25.8 2.5 copy.39
  28.3 6.1 %rev.15 = bf16[256,64,64]{0,2,1:T(8,128)(2,1)} reverse(bf16[256,64,64]{0,2,1:T(8,128)(2,1)} %bitcast.89), dimensions={0} | reverse | bytes 4194304 | tf_op jit(solution)/shard_map/rev | solution.py:139
  34.4 3.8 fusion.39
  41.5 4.1 %copy.34 = bf16[256,4096]{0,1:T(8,128)(2,1)} copy(bf16[256,4096]{1,0:T(8,128)(2,1)} %slice.132) | data formatting | bytes 4194304 | tf_op jit(solution)/shard_map/slice | solution.py:62
  45.6 3.6 fusion.36
  49.4 13.8 %all-gather.2 = f32[8,64,1]{1,2,0:T(1,128)S(1)} all-gather(f32[1,64,1]{1,2,0:T(1,128)S(1)} %copy.43), channel_id=4, replica_groups=mesh['row'=4,'seq'=8] {'seq'}, dimensions={0}, use_global_device_ids=true | all-gather | bytes 2304 | tf_op jit(solution)/shard_map/all_gather | solution.py:32
  63.2 12.9 %all-gather = f32[8,64,1]{1,2,0:T(1,128)S(1)} all-gather(f32[1,64,1]{1,2,0:T(1,128)S(1)} %copy.38), channel_id=2, replica_groups=mesh['row'=4,'seq'=8] {'seq'}, dimensions={0}, use_global_device_ids=true | all-gather | bytes 2304 | tf_op jit(solution)/shard_map/all_gather | solution.py:32
  77.5 114.8 %all-gather.9.cloned.1.call-done = f32[512,64,128]{2,1,0:T(8,128)} async-done(((f32[64,64,128]{2,1,0:T(8,128)}), f32[512,64,128]{2,1,0:T(8,128)}) %all-gather.9.cloned.1.call-update) | async-done | bytes 16777232 | tf_op jit(solution)/shard_map/all_gather | solution.py:32
  192.3 31.7 %while.21 = (s32[]{:T(128)}, f32[64,64,128]{2,1,0:T(8,128)}, s32[]{:T(128)}, f32[8,64]{1,0:T(8,128)S(1)}, f32[8,64,64,128]{3,2,1,0:T(8,128)}, /*index=5*/s32[]{:T(128)}, s32[]{:T(128)}, s32[]{:T(128)}, s32[]{:T(128)}) while((s32[]{:T(128)}, f32[64,64,128]{2,1,0:T(8,128)}, s32[]{:T(128)}, f32[8,64]{1,0:T(8,128)S(1)}, ...), condition=%wide.region_7.8_spmd.clone, body=%wide.region_6.7_spmd.clone.sunk | while | flops 2097160 | bytes 6292399 | solution.py:45
  192.3 3.2 fusion.69
  195.5 3.9 fusion.69
  199.4 4.6 %fusion.69 = f32[64,64,128]{2,1,0:T(8,128)} fusion(f32[8,64,64,128]{3,2,1,0:T(8,128)} %get-tuple-element.485, s32[]{:T(128)S(6)} %select_n.90, f32[64,64,128]{2,1,0:T(8,128)} %get-tuple-element.473, f32[64]{0:T(128)S(1)} %dynamic-slice_bitcast_fusion.5, pred[]{:T(512)S(6)} %compare.7, pred[]{:T(512)S(6)} %gt.12), kind=kLoop, calls=%fused_computation.4.clone.1 | loop fusion | flops 2097152 | bytes 6291718 | tf_op jit(solution)/shard_map/while/body/eval_jaxpr/jit(_where)/select_n | solution.py:43
  204.0 4.5 %fusion.69 = f32[64,64,128]{2,1,0:T(8,128)} fusion(f32[8,64,64,128]{3,2,1,0:T(8,128)} %get-tuple-element.485, s32[]{:T(128)S(6)} %select_n.90, f32[64,64,128]{2,1,0:T(8,128)} %get-tuple-element.473, f32[64]{0:T(128)S(1)} %dynamic-slice_bitcast_fusion.5, pred[]{:T(512)S(6)} %compare.7, pred[]{:T(512)S(6)} %gt.12), kind=kLoop, calls=%fused_computation.4.clone.1 | loop fusion | flops 2097152 | bytes 6291718 | tf_op jit(solution)/shard_map/while/body/eval_jaxpr/jit(_where)/select_n | solution.py:43
  208.4 3.9 fusion.69
  212.3 3.9 %fusion.69 = f32[64,64,128]{2,1,0:T(8,128)} fusion(f32[8,64,64,128]{3,2,1,0:T(8,128)} %get-tuple-element.485, s32[]{:T(128)S(6)} %select_n.90, f32[64,64,128]{2,1,0:T(8,128)} %get-tuple-element.473, f32[64]{0:T(128)S(1)} %dynamic-slice_bitcast_fusion.5, pred[]{:T(512)S(6)} %compare.7, pred[]{:T(512)S(6)} %gt.12), kind=kLoop, calls=%fused_computation.4.clone.1 | loop fusion | flops 2097152 | bytes 6291718 | tf_op jit(solution)/shard_map/while/body/eval_jaxpr/jit(_where)/select_n | solution.py:43
  216.2 3.9 fusion.69
  220.1 3.9 fusion.69
  224.0 3.7 fusion.30
  227.7 6.3 %bitcast_add_fusion.2 = f32[256,64,64]{0,2,1:T(8,128)} fusion(f32[256,64,64]{0,2,1:T(8,128)S(1)} %fusion.30, bf16[256,64,64]{0,2,1:T(8,128)(2,1)S(1)} %copy-done.4, f32[64,256]{1,0:T(8,128)S(1)} %rev.18, f32[64,256]{1,0:T(8,128)S(1)} %copy_bitcast_fusion, f32[256,256]{1,0:T(8,128)S(1)} %fusion.55, pred[256,256]{1,0:T(8,128)(4,1)S(1)} %iota_compare_fusion, ...), kind=kOutput, calls=%fused_computation.38 | convolution fusion | flops 559939584 | bytes 11010048 | tf_op jit(solution)/shard_map/while/body/eval_jaxpr/hts,shp->thp/dot_general | solution.py:77
  233.9 7.3 %rev.19 = f32[256,64,64]{0,2,1:T(8,128)} reverse(f32[256,64,64]{0,2,1:T(8,128)} %bitcast_add_fusion.2), dimensions={0} | reverse | bytes 8388608 | tf_op jit(solution)/shard_map/rev | solution.py:145
  241.2 102.0 %all-gather.7.cloned.1.call-done = f32[512,64,128]{2,1,0:T(8,128)} async-done(((f32[64,64,128]{2,1,0:T(8,128)}), f32[512,64,128]{2,1,0:T(8,128)}) %all-gather.7.cloned.1.call-update) | async-done | bytes 16777232 | tf_op jit(solution)/shard_map/all_gather | solution.py:32
  343.2 17.0 %while.20 = (s32[]{:T(128)}, f32[64,64,128]{2,1,0:T(8,128)S(1)}, s32[]{:T(128)}, f32[8,64]{1,0:T(8,128)S(1)}, f32[8,64,64,128]{3,2,1,0:T(8,128)}, /*index=5*/s32[]{:T(128)}, s32[]{:T(128)}) while((s32[]{:T(128)}, f32[64,64,128]{2,1,0:T(8,128)S(1)}, s32[]{:T(128)}, f32[8,64]{1,0:T(8,128)S(1)}, f32[8,64,64,128]{3,2,1,0:T(8,128)}, ...), condition=%wide.region_3.4_spmd.clone, body=%wide.region_2.3_spmd.clone.sunk | while | flops 2097156 | bytes 6292337 | solution.py:45
  345.4 2.1 fusion.68
  347.5 2.1 fusion.68
  349.6 2.1 fusion.68
  360.2 2.8 fusion.33
  363.1 6.6 %fusion.19 = f32[256,64,64]{0,2,1:T(8,128)} fusion(bf16[256,64,64]{0,2,1:T(8,128)(2,1)S(1)} %bitcast.88, f32[256,64,64]{0,2,1:T(8,128)S(1)} %copy-done.5, f32[256,64,64]{0,2,1:T(8,128)S(1)} %fusion.33, f32[64,256]{1,0:T(8,128)S(1)} %copy-done.6, f32[64,256]{1,0:T(8,128)S(1)} %copy_bitcast_fusion.1, f32[256,256]{1,0:T(8,128)S(1)} %fusion.47, ...), kind=kOutput, calls=%fused_computation.33 | convolution fusion | flops 564133888 | bytes 15204608 | tf_op jit(solution)/shard_map/while/body/eval_jaxpr/hts,shp->thp/dot_general | solution.py:77
  369.7 5.8 %copy.44 = f32[256,4096]{1,0:T(8,128)} copy(f32[256,4096]{0,1:T(8,128)} %bitcast.92) | data formatting | bytes 8388608 | tf_op jit(solution)/shard_map/reshape | solution.py:147
  375.5 3.9 multiply_reduce_fusion
  379.4 3.1 multiply_convert_fusion.6
  (97 shorter events, 21.9 us)
Async XLA Ops:
  6.5 7.2 %copy-start.10 = (f32[64]{0:T(128)S(1)}, f32[64]{0:T(128)}, u32[]{:S(2)}) copy-start(f32[64]{0:T(128)} %param.17) | copy-start | bytes 772
  6.5 7.2 %copy-start.6 = (f32[64,256]{1,0:T(8,128)S(1)}, f32[64,256]{1,0:T(8,128)}, u32[]{:S(2)}) copy-start(f32[64,256]{1,0:T(8,128)} %param.16) | copy-start | bytes 196612
  6.5 9.1 %copy-start.7 = (f32[4,4352]{1,0:T(4,128)S(1)}, f32[4,4352]{1,0:T(4,128)}, u32[]{:S(2)}) copy-start(f32[4,4352]{1,0:T(4,128)} %param.15) | copy-start | bytes 208900
  6.5 9.1 %copy-start.8 = (f32[4,4352]{1,0:T(4,128)S(1)}, f32[4,4352]{1,0:T(4,128)}, u32[]{:S(2)}) copy-start(f32[4,4352]{1,0:T(4,128)} %param.14) | copy-start | bytes 208900
  6.5 185.7 %all-gather.9.cloned.1.call-start = ((), (), s32[]{:S(2)}) async-start(), calls=%async_computation.1 | async-start | bytes 18874368 | tf_op jit(solution)/shard_map/all_gather | solution.py:32
  7.6 8.4 %collective-permute-start.1 = (bf16[3,4352]{1,0:T(4,128)(2,1)S(1)}, bf16[3,4352]{1,0:T(4,128)(2,1)S(1)}, u32[]{:S(2)}, u32[]{:S(2)}) collective-permute-start(bf16[3,4352]{1,0:T(4,128)(2,1)S(1)} %get-tuple-element.389), channel_id=1, source_target_pairs={{1,0},{2,1},{3,2},{4,3},{5,4},{6,5},{7,6},{9,8},{10,9},{11,10},{12... | collective-permute-start | bytes 78344 | tf_op jit(solution)/shard_map/ppermute | solution.py:23
  8.9 7.2 %collective-permute-start = (bf16[3,4352]{1,0:T(4,128)(2,1)S(1)}, bf16[3,4352]{1,0:T(4,128)(2,1)S(1)}, u32[]{:S(2)}, u32[]{:S(2)}) collective-permute-start(bf16[3,4352]{1,0:T(4,128)(2,1)S(1)} %get-tuple-element.390), channel_id=1, source_target_pairs={{0,1},{1,2},{2,3},{3,4},{4,5},{5,6},{6,7},{8,9},{9,10},{10,11},{11... | collective-permute-start | bytes 78344 | tf_op jit(solution)/shard_map/ppermute | solution.py:21
  34.3 5.6 %copy-start.1 = (bf16[256,4352]{1,0:T(8,128)(2,1)S(1)}, bf16[256,4352]{1,0:T(8,128)(2,1)}, u32[]{:S(2)}) copy-start(bf16[256,4352]{1,0:T(8,128)(2,1)} %get-tuple-element.388) | copy-start | bytes 6684676
  38.2 305.0 %all-gather.7.cloned.1.call-start = ((), (), s32[]{:S(2)}) async-start(), calls=%async_computation | async-start | bytes 18874368 | tf_op jit(solution)/shard_map/all_gather | solution.py:32
  224.0 3.7 copy-start.4
  360.2 2.9 copy-start.3
  360.2 2.9 copy-start.5
  360.2 2.9 copy-start.11
  369.7 5.8 %copy-start.2 = (bf16[256,4096]{1,0:T(8,128)(2,1)S(1)}, bf16[256,4096]{1,0:T(8,128)(2,1)}, u32[]{:S(2)}) copy-start(bf16[256,4096]{1,0:T(8,128)(2,1)} %param.13) | copy-start | bytes 6291460
  375.5 3.9 copy-start
  375.5 3.9 copy-start.9
Sparse Core Ops, SparseCore 0:
  38.4 153.8 all-gather.8
  193.9 149.3 all-gather.6
where the time goes:
time: 390 us; the launch traced here: 389 us
  waiting for transfers between devices  217 us (56%)
  other arithmetic  67 us (17%)
  local copies, waits for them, and re-layouts  32.3 us (8%)
  matrix products  28 us (7%)
  blocking collectives  26.7 us (7%)
  between operations  13.8 us (4%)
  starting transfers between devices  4.4 us (1%)
    all_gather x2, waiting for transfers between devices, entering(): everything = jax.tree.map(lambda part: lax.all_gather(part, axis), array)  217 us
    select_n x16, other arithmetic, lap(): return jax.tree.map(lambda a, b: jnp.where(reached, a, b), new, before)  48.3 us
    all_gather x2, blocking collectives, entering(): everything = jax.tree.map(lambda part: lax.all_gather(part, axis), array)  26.7 us
    dot_general x2, matrix products, block_terms(): jnp.einsum('hts,shp->thp', scores, block_values, preferred_element_type=j...  12.9 us
    convert_element_type x1, other arithmetic, conv_pair(): jax.nn.silu(behind).astype(jnp.bfloat16)  9.44 us
    slice x4, local copies, waits for them, and re-layouts, split_pieces(): values = convolved[:, :inner].reshape(length, HEADS, HEAD_DIM)  8.37 us
  transfers between devices with their start and end apart: 4, of which 2 were waited for; matrix products, arithmetic and copies ran while one was open for 17% of the time, Pallas kernels for 0%

commit v1 on v0

v1 whole, which is shorter than its diff:
```python
import functools

import jax
import jax.numpy as jnp
from jax import lax
from jax.experimental import pallas as pl
from jax.experimental.pallas import tpu as pltpu
from jax.sharding import PartitionSpec as P

HEADS = 64
HEAD_DIM = 64
STATE = 128
WIDTH = 4
BLOCK = 256
INNER = HEADS * HEAD_DIM
PIECE = 256
PIECES = INNER // PIECE
PER = PIECE // HEAD_DIM
HALO = 16
STRIP = 64
LAG = 2
LOG2E = 1.4426950408889634
F32 = jnp.float32
BF16 = jnp.bfloat16
MESH = pl.DeviceIdType.MESH


def dot(a, b):
    return jnp.dot(a, b, preferred_element_type=F32)


def silu(x):
    y = 0.5 * x
    return y + y * jnp.tanh(y)


def kernel(
    n,
    x_hbm, gate_hbm, tapf, tapr, step_ref, decay, skip, gain, out_hbm,
    xpad, gate_v, va, vb, acc, sg, stf, str_, cinf, cinr, sbf, sbr,
    colc, cfs, ces, rowc, aft, sel, drow, gf_ref, gr_ref, kq, kt, ssq, out_v,
    local_sem, halo_send, halo_recv, sendf, recvf, sendr, recvr, out_sem,
):
    me = lax.axis_index("seq")
    has_left = me > 0
    has_right = me < n - 1
    left = lax.rem(me + n - 1, n)
    right = lax.rem(me + 1, n)

    load_x = pltpu.make_async_copy(x_hbm, xpad.at[pl.ds(HALO, BLOCK)], local_sem.at[0])
    load_gate = pltpu.make_async_copy(gate_hbm, gate_v, local_sem.at[1])
    load_x.start()
    load_gate.start()

    barrier = pltpu.get_barrier_semaphore()

    @pl.when(has_left)
    def _():
        pl.semaphore_signal(barrier, inc=1, device_id={"seq": left}, device_id_type=MESH)

    @pl.when(has_right)
    def _():
        pl.semaphore_signal(barrier, inc=1, device_id={"seq": right}, device_id_type=MESH)

    pl.semaphore_wait(barrier, has_left.astype(jnp.int32) + has_right.astype(jnp.int32))

    to_right = pltpu.make_async_remote_copy(
        src_ref=x_hbm.at[pl.ds(BLOCK - HALO, HALO)],
        dst_ref=xpad.at[pl.ds(0, HALO)],
        send_sem=halo_send.at[0],
        recv_sem=halo_recv.at[0],
        device_id={"seq": right},
        device_id_type=MESH,
    )
    to_left = pltpu.make_async_remote_copy(
        src_ref=x_hbm.at[pl.ds(0, HALO)],
        dst_ref=xpad.at[pl.ds(HALO + BLOCK, HALO)],
        send_sem=halo_send.at[1],
        recv_sem=halo_recv.at[1],
        device_id={"seq": left},
        device_id_type=MESH,
    )

    @pl.when(has_right)
    def _():
        to_right.start()

    @pl.when(has_left)
    def _():
        to_left.start()

    @pl.when(jnp.logical_not(has_left))
    def _():
        xpad[0:HALO, :] = jnp.zeros((HALO, xpad.shape[1]), BF16)

    @pl.when(jnp.logical_not(has_right))
    def _():
        xpad[HALO + BLOCK :, :] = jnp.zeros((HALO, xpad.shape[1]), BF16)

    for h in range(HEADS):
        ces[h : h + 1, :] = step_ref[h : h + 1, :] * (decay[h] * -LOG2E)
    logs = ces[...]
    row_i = lax.broadcasted_iota(jnp.int32, (BLOCK, BLOCK), 0)
    col_i = lax.broadcasted_iota(jnp.int32, (BLOCK, BLOCK), 1)
    upto = jnp.where(row_i <= col_i, 1.0, 0.0).astype(F32)
    cum = jnp.dot(logs, upto, preferred_element_type=F32, precision=lax.Precision.HIGHEST)
    before = cum - logs
    total = cum[:, BLOCK - 1 : BLOCK]
    steps = step_ref[...]
    log_steps = jnp.log(steps) * LOG2E
    cfs[...] = cum - log_steps
    ces[...] = before + log_steps
    for p in range(PIECES):
        rowc[p, 0:PER, :] = cfs[p * PER : (p + 1) * PER, :]
        rowc[p, PER : 2 * PER, :] = ces[p * PER : (p + 1) * PER, :]
    columns = jnp.transpose(jnp.concatenate([cum, before], axis=0))
    for p in range(PIECES):
        shift = (STATE - PER * p) % STATE
        colc[p] = pltpu.roll(columns, shift, axis=1) if shift else columns
    factors = (
        steps * jnp.exp2(total - cum),
        steps * jnp.exp2(before),
        jnp.exp2(cum),
        jnp.exp2(total - before),
    )
    parts = []
    for f in factors:
        high = f.astype(BF16).astype(F32)
        parts.append((high, f - high))
    for v in range(PIECES // 4):
        rows = []
        for u in (2 * v, 2 * v + 1):
            for high, low in parts:
                rows.append(high[8 * u : 8 * u + 8])
                rows.append(low[8 * u : 8 * u + 8])
        aft[v] = jnp.transpose(jnp.concatenate(rows, axis=0)).astype(BF16)
    sel_row = lax.broadcasted_iota(jnp.int32, (STATE, PIECE), 0)
    sel_col = lax.broadcasted_iota(jnp.int32, (STATE, PIECE), 1) // HEAD_DIM
    base = sel_row - sel_col
    for q in range(4):
        for f in range(4):
            off = (q // 2) * 64 + f * 16 + (q % 2) * 4
            hit = jnp.logical_or(base == off, base == off + 8)
            sel[q, :, f * PIECE : (f + 1) * PIECE] = jnp.where(hit, 1.0, 0.0).astype(BF16)

    load_x.wait()

    @pl.when(has_right)
    def _():
        to_right.wait_send()
        to_left.wait_recv()

    @pl.when(has_left)
    def _():
        to_right.wait_recv()
        to_left.wait_send()

    def conv(r, cols):
        xs = xpad[pl.ds(r, STRIP + 2 * HALO), cols].astype(F32)
        ahead = behind = None
        rows = STRIP + 2 * HALO

        def at(d):
            moved = xs if d == 0 else pltpu.roll(xs, (-d) % rows, axis=0)
            return moved[HALO : HALO + STRIP]

        fw = tapf[:, cols]
        rv = tapr[:, cols]
        for k in range(WIDTH):
            a = fw[k : k + 1] * at(k - (WIDTH - 1))
            b = rv[k : k + 1] * at(WIDTH - 1 - k)
            ahead = a if ahead is None else ahead + a
            behind = b if behind is None else behind + b
        return silu(ahead).astype(BF16), silu(behind).astype(BF16)

    for which in range(2):
        for r in range(0, BLOCK, STRIP):
            a, b = conv(r, pl.ds(INNER + which * STATE, STATE))
            kq[which, r : r + STRIP, :] = a
            kq[2 + which, r : r + STRIP, :] = b
    kt[0] = jnp.transpose(kq[0].astype(F32)).astype(BF16)
    kt[1] = jnp.transpose(kq[2].astype(F32)).astype(BF16)
    gf_ref[...] = jnp.where(row_i >= col_i, dot(kq[1], kt[0]), 0.0)
    gr_ref[...] = jnp.where(row_i <= col_i, dot(kq[3], kt[1]), 0.0)
    load_gate.wait()

    lane = lax.broadcasted_iota(jnp.int32, (1, STATE), 1)
    first_half = lane < HEAD_DIM

    def make(p):
        v = p // 4
        q = lax.rem(p, 4)
        for c in range(PIECE // STATE):
            cols = pl.ds(pl.multiple_of(p * PIECE + c * STATE, STATE), STATE)
            skip_row = jnp.where(first_half, skip[p * PER + 2 * c], skip[p * PER + 2 * c + 1])
            for r in range(0, BLOCK, STRIP):
                a, b = conv(r, cols)
                here = (p, pl.ds(r, STRIP), pl.ds(c * STATE, STATE))
                va[here] = a
                vb[here] = b
                acc[here] = skip_row * a.astype(F32)
        wide = dot(aft[v], sel[q, :, 0 : 2 * PIECE])
        wf = (va[p].astype(F32) * wide[:, :PIECE]).astype(BF16)
        stf[p] = dot(kt[0], wf)
        wr = (vb[p].astype(F32) * wide[:, PIECE:]).astype(BF16)
        str_[p] = dot(kt[1], wr)
        ends = dot(aft[v, BLOCK - 16 : BLOCK, :], sel[q, :, 2 * PIECE : 3 * PIECE])
        drow[p, 0:1, :] = ends[15:16, :]

    def hop(p, forward):
        cin, sb, st = (cinf, sbf, stf) if forward else (cinr, sbr, str_)
        send, recv = (sendf, recvf) if forward else (sendr, recvr)
        takes, gives = (has_left, has_right) if forward else (has_right, has_left)
        target = right if forward else left
        copy = pltpu.make_async_remote_copy(
            src_ref=sb.at[p],
            dst_ref=cin.at[p],
            send_sem=send.at[p],
            recv_sem=recv.at[p],
            device_id={"seq": target},
            device_id_type=MESH,
        )
        return copy, cin, sb, st, takes, gives

    def chain(p, forward):
        copy, cin, sb, st, takes, gives = hop(p, forward)

        @pl.when(takes)
        def _():
            copy.wait_recv()

            @pl.when(gives)
            def _():
                sb[p] = (st[p] + drow[p, 0:1, :] * cin[p].astype(F32)).astype(BF16)

        @pl.when(jnp.logical_not(takes))
        def _():
            sb[p] = st[p].astype(BF16)

        @pl.when(gives)
        def _():
            copy.start()

        @pl.when(takes)
        def _():
            first = (2 if forward else 3) * PIECE
            grow = dot(aft[p // 4], sel[lax.rem(p, 4), :, first : first + PIECE])
            acc[p] = acc[p] + grow * dot(kq[1 if forward else 3], cin[p])

    half = BLOCK // 2

    def within(p):
        for pair in range(PER // 2):
            lanes = slice(pair * STATE, (pair + 1) * STATE)
            vf = va[p, :, lanes]
            vr = vb[p, :, lanes]
            res = []
            for j in (2 * pair, 2 * pair + 1):
                cft = colc[p, :, j : j + 1]
                cet = colc[p, :, 64 + j : 65 + j]
                ra = rowc[p, j : j + 1, :]
                rb = rowc[p, PER + j : PER + j + 1, :]
                lo, hi = slice(0, half), slice(half, BLOCK)
                d00 = jnp.exp2(jnp.minimum(cft[lo] - ra[:, lo], rb[:, lo] - cet[lo]))
                d01 = jnp.exp2(rb[:, hi] - cet[lo])
                f00 = (gf_ref[lo, lo] * d00).astype(BF16)
                r00 = (gr_ref[lo, lo] * d00).astype(BF16)
                r01 = (gr_ref[lo, hi] * d01).astype(BF16)
                top = dot(f00, vf[lo]) + dot(jnp.concatenate([r00, r01], axis=1), vr)
                d11 = jnp.exp2(jnp.minimum(cft[hi] - ra[:, hi], rb[:, hi] - cet[hi]))
                d10 = jnp.exp2(cft[hi] - ra[:, lo])
                f10 = (gf_ref[hi, lo] * d10).astype(BF16)
                f11 = (gf_ref[hi, hi] * d11).astype(BF16)
                r11 = (gr_ref[hi, hi] * d11).astype(BF16)
                low = dot(jnp.concatenate([f10, f11], axis=1), vf) + dot(r11, vr[hi])
                res.append((top, low))
            for i, rows in enumerate((slice(0, half), slice(half, BLOCK))):
                acc[p, rows, lanes] = acc[p, rows, lanes] + jnp.where(
                    first_half, res[0][i], res[1][i]
                )
        for r in range(0, BLOCK, STRIP):
            g = gate_v[r : r + STRIP, pl.ds(pl.multiple_of(p * PIECE, PIECE), PIECE)]
            sg[p, r : r + STRIP, :] = silu(g.astype(F32))

    def slot(k, carry):
        kf = k - LAG * me
        kr = k - LAG * (n - 1 - me)
        kw = k - PIECES

        @pl.when(k < PIECES)
        def _():
            make(k)

        @pl.when(jnp.logical_and(kf >= 0, kf < PIECES))
        def _():
            chain(kf, True)

        @pl.when(jnp.logical_and(kr >= 0, kr < PIECES))
        def _():
            chain(kr, False)

        @pl.when(jnp.logical_and(kw >= 0, kw < PIECES))
        def _():
            within(kw)

        return carry

    lax.fori_loop(0, PIECES + max(LAG * (n - 1), PIECES), slot, 0)

    ssq[...] = jnp.zeros_like(ssq)

    def gather(p, carry):
        for r in range(0, BLOCK, STRIP):
            rows = pl.ds(r, STRIP)
            y = acc[p, rows, :] * sg[p, rows, :]
            acc[p, rows, :] = y
            y = y * y
            ssq[rows, :] = ssq[rows, :] + (y[:, :STATE] + y[:, STATE:])
        return carry

    lax.fori_loop(0, PIECES, gather, 0)
    scale = lax.rsqrt(jnp.sum(ssq[...], axis=1, keepdims=True) * (1.0 / INNER) + 1e-05)
    ssq[...] = jnp.broadcast_to(scale, ssq.shape)

    copies = []
    for i, r in enumerate(range(0, BLOCK, STRIP)):
        rows = pl.ds(r, STRIP)

        def emit(p, carry):
            cols = pl.ds(pl.multiple_of(p * PIECE, PIECE), PIECE)
            s = ssq[rows, :]
            s = jnp.concatenate([s, s], axis=1)
            out_v[rows, cols] = (acc[p, rows, :] * s * gain[:, cols]).astype(BF16)
            return carry

        lax.fori_loop(0, PIECES, emit, 0)
        copy = pltpu.make_async_copy(out_v.at[rows], out_hbm.at[rows], out_sem.at[i])
        copy.start()
        copies.append(copy)

    @pl.when(has_right)
    def _():
        def done(p, carry):
            hop(p, True)[0].wait_send()
            return carry

        lax.fori_loop(0, PIECES, done, 0)

    @pl.when(has_left)
    def _():
        def done(p, carry):
            hop(p, False)[0].wait_send()
            return carry

        lax.fori_loop(0, PIECES, done, 0)

    for copy in copies:
        copy.wait()


def per_device(
    mixer_input, gate_input, conv_forward, conv_reverse, step_size, decay_rate, skip_scale, norm_gain
):
    n = lax.axis_size("seq")
    vmem = pl.BlockSpec(memory_space=pltpu.VMEM)
    smem = pl.BlockSpec(memory_space=pltpu.SMEM)
    hbm = pl.BlockSpec(memory_space=pl.ANY)
    piece = (PIECES, BLOCK, PIECE)
    state = (PIECES, STATE, PIECE)
    dma = pltpu.SemaphoreType.DMA
    return pl.pallas_call(
        functools.partial(kernel, n),
        out_shape=jax.ShapeDtypeStruct((BLOCK, INNER), BF16),
        in_specs=[hbm, hbm, vmem, vmem, vmem, smem, smem, vmem],
        out_specs=hbm,
        scratch_shapes=[
            pltpu.VMEM((BLOCK + 2 * HALO, INNER + 2 * STATE), BF16),
            pltpu.VMEM((BLOCK, INNER), BF16),
            pltpu.VMEM(piece, BF16),
            pltpu.VMEM(piece, BF16),
            pltpu.VMEM(piece, F32),
            pltpu.VMEM(piece, F32),
            pltpu.VMEM(state, F32),
            pltpu.VMEM(state, F32),
            pltpu.VMEM(state, BF16),
            pltpu.VMEM(state, BF16),
            pltpu.VMEM(state, BF16),
            pltpu.VMEM(state, BF16),
            pltpu.VMEM((PIECES, BLOCK, STATE), F32),
            pltpu.VMEM((HEADS, BLOCK), F32),
            pltpu.VMEM((HEADS, BLOCK), F32),
            pltpu.VMEM((PIECES, 2 * PER, BLOCK), F32),
            pltpu.VMEM((PIECES // 4, BLOCK, STATE), BF16),
            pltpu.VMEM((4, STATE, 4 * PIECE), BF16),
            pltpu.VMEM((PIECES, 8, PIECE), F32),
            pltpu.VMEM((BLOCK, BLOCK), F32),
            pltpu.VMEM((BLOCK, BLOCK), F32),
            pltpu.VMEM((4, BLOCK, STATE), BF16),
            pltpu.VMEM((2, STATE, BLOCK), BF16),
            pltpu.VMEM((BLOCK, STATE), F32),
            pltpu.VMEM((BLOCK, INNER), BF16),
            dma((2,)),
            dma((2,)),
            dma((2,)),
            dma((PIECES,)),
            dma((PIECES,)),
            dma((PIECES,)),
            dma((PIECES,)),
            dma((BLOCK // STRIP,)),
        ],
        compiler_params=pltpu.CompilerParams(
            collective_id=0, has_side_effects=True, vmem_limit_bytes=56 * 1024 * 1024
        ),
        cost_estimate=pl.CostEstimate(flops=3 * 10**9, bytes_accessed=7 * 10**6, transcendentals=10**7),
        name="mixer",
    )(
        mixer_input, gate_input, conv_forward, conv_reverse, step_size, decay_rate, skip_scale,
        norm_gain.reshape(1, INNER),
    )


def solution(mesh):
    in_specs = (
        P(("row", "seq"), None),
        P(("row", "seq"), None),
        P(),
        P(),
        P(None, ("row", "seq")),
        P("row"),
        P(),
        P(),
    )
    out_specs = P(("row", "seq"), None)
    return jax.shard_map(
        per_device, mesh=mesh, in_specs=in_specs, out_specs=out_specs, check_vma=False
    )
```

time: 390 us -> 52.6 us (0.13)
  waiting for transfers between devices: 217 us -> 0 us
  other arithmetic: 67 us -> 0 us
  Pallas kernels: 0 us -> 49.3 us
  local copies, waits for them, and re-layouts: 32.3 us -> 3.13 us
  matrix products: 28 us -> 0 us
  blocking collectives: 26.7 us -> 0 us
  between operations: 13.8 us -> 0.01 us
  starting transfers between devices: 4.4 us -> 0 us
    all_gather x2 -> x0, waiting for transfers between devices: 217 us -> none  [entering(): everything = jax.tree.map(lambda part: lax.all_gather(part, axis), array)]
    pallas_call x0 -> x1, Pallas kernels: none -> 49.3 us  [per_device(): pl.pallas_call(functools.partial(kernel, n), out_shape=jax.ShapeDtypeStru...]
    select_n x16 -> x0, other arithmetic: 48.3 us -> none  [lap(): return jax.tree.map(lambda a, b: jnp.where(reached, a, b), new, before)]
    dot_general x8 -> x0, matrix products: 28 us -> none  [the longest x2 12.9 us: block_terms(): jnp.einsum('hts,shp->thp', scores, block_values, preferred_element_type=j...]
    all_gather x2 -> x0, blocking collectives: 26.7 us -> none  [entering(): everything = jax.tree.map(lambda part: lax.all_gather(part, axis), array)]
    rev x5 -> x0, local copies, waits for them, and re-layouts: 13.7 us -> none  [the longest x1 7.27 us: per_device(): reverse = finish(reverse_parts, reverse_in)[::-1]]
    convert_element_type x2 -> x0, other arithmetic: 12.5 us -> none  [the longest x1 9.44 us: conv_pair(): jax.nn.silu(behind).astype(jnp.bfloat16)]
    slice x9 -> x0, local copies, waits for them, and re-layouts: 10.1 us -> none  [the longest x4 8.37 us: split_pieces(): values = convolved[:, :inner].reshape(length, HEADS, HEAD_DIM)]
  transfers between devices with their start and end apart: 4 -> 0, of which waited for: 2 -> 0; matrix products, arithmetic and copies ran while one was open for 17% -> 0% of each run, Pallas kernels for 0% -> 0%
where the time goes in v1:
time: 52.6 us; the launch traced here: 52.4 us
  Pallas kernels  49.3 us (94%)
  local copies, waits for them, and re-layouts  3.13 us (6%)
    pallas_call x1, Pallas kernels, per_device(): pl.pallas_call(functools.partial(kernel, n), out_shape=jax.ShapeDtypeStru...  49.3 us
    unnamed x1, local copies, waits for them, and re-layouts  3.13 us

profile of v1, /device:TPU:0, one launch (start us, length us, event | category | flops | bytes accessed | tf_op | source)
XLA Modules:
  0.0 52.4 jit_solution(3138005542031825945)
XLA Ops:
  0.0 49.3 %mixer.1 = bf16[256,4096]{1,0:T(8,128)(2,1)} custom-call(bf16[256,4352]{1,0:T(8,128)(2,1)} %x_hbm.1, bf16[256,4096]{1,0:T(8,128)(2,1)} %gate_hbm.1, f32[4,4352]{1,0:T(4,128)} %tapf.1, f32[4,4352]{1,0:T(4,128)} %tapr.1, f32[64,256]{1,0:T(8,128)} %step_ref.1, f32[64]{0:T(128)} %decay.1, f32[64]{0:T(128)} %skip.1, f32[1,4096]{1,0:T(1,128)} %bitcast.1), custom_call_target="tpu_custom_call" | custom-call | flops 3000000000 | bytes 7000000 | tf_op jit(solution)/shard_map/mixer/pallas_call | solution.py:371
  49.3 3.1 %copy.10 = bf16[256,4096]{1,0:T(8,128)(2,1)} copy(bf16[256,4096]{1,0:T(8,128)(2,1)} %mixer.1) | data formatting | bytes 4194304

commit v2 on v1

--- a/solution.py
+++ b/solution.py
@@ -18,7 +18,7 @@
 PER = PIECE // HEAD_DIM
 HALO = 16
 STRIP = 64
-LAG = 2
+LAG = 4
 LOG2E = 1.4426950408889634
 F32 = jnp.float32
 BF16 = jnp.bfloat16
@@ -36,9 +36,9 @@
 
 def kernel(
     n,
-    x_hbm, gate_hbm, tapf, tapr, step_ref, decay, skip, gain, out_hbm,
-    xpad, gate_v, va, vb, acc, sg, stf, str_, cinf, cinr, sbf, sbr,
-    colc, cfs, ces, rowc, aft, sel, drow, gf_ref, gr_ref, kq, kt, ssq, out_v,
+    x_hbm, gate_hbm, tapf, tapr, step_ref, decay, skip, y_hbm, scale_ref,
+    xpad, gate_v, vcat, accw, accf, accr, stf, str_, cinf, cinr, sbf, sbr,
+    colc, cfs, ces, rowc, aft, sel, drow, gf_ref, gr_ref, kq, kt, ssq, y_v,
     local_sem, halo_send, halo_recv, sendf, recvf, sendr, recvr, out_sem,
 ):
     me = lax.axis_index("seq")
@@ -143,6 +143,7 @@
             hit = jnp.logical_or(base == off, base == off + 8)
             sel[q, :, f * PIECE : (f + 1) * PIECE] = jnp.where(hit, 1.0, 0.0).astype(BF16)
 
+    half = BLOCK // 2
     load_x.wait()
 
     @pl.when(has_right)
@@ -156,13 +157,13 @@
         to_left.wait_send()
 
     def conv(r, cols):
-        xs = xpad[pl.ds(r, STRIP + 2 * HALO), cols].astype(F32)
+        xs = xpad[pl.ds(r, STRIP + 2 * HALO), cols].astype(F32)[8 : STRIP + 24]
         ahead = behind = None
-        rows = STRIP + 2 * HALO
+        rows = STRIP + 16
 
         def at(d):
             moved = xs if d == 0 else pltpu.roll(xs, (-d) % rows, axis=0)
-            return moved[HALO : HALO + STRIP]
+            return moved[8 : 8 + STRIP]
 
         fw = tapf[:, cols]
         rv = tapr[:, cols]
@@ -178,10 +179,13 @@
             a, b = conv(r, pl.ds(INNER + which * STATE, STATE))
             kq[which, r : r + STRIP, :] = a
             kq[2 + which, r : r + STRIP, :] = b
-    kt[0] = jnp.transpose(kq[0].astype(F32)).astype(BF16)
-    kt[1] = jnp.transpose(kq[2].astype(F32)).astype(BF16)
-    gf_ref[...] = jnp.where(row_i >= col_i, dot(kq[1], kt[0]), 0.0)
-    gr_ref[...] = jnp.where(row_i <= col_i, dot(kq[3], kt[1]), 0.0)
+    lo, hi = slice(0, half), slice(half, BLOCK)
+    for i in range(2):
+        keys = jnp.transpose(kq[2 * i].astype(F32)).astype(BF16)
+        kt[i, :, lo] = keys[:, hi]
+        kt[i, :, hi] = keys[:, lo]
+        inside = row_i >= col_i if i == 0 else row_i <= col_i
+        (gf_ref, gr_ref)[i][...] = jnp.where(inside, dot(kq[2 * i + 1], keys), 0.0)
     load_gate.wait()
 
     lane = lax.broadcasted_iota(jnp.int32, (1, STATE), 1)
@@ -192,20 +196,35 @@
         q = lax.rem(p, 4)
         for c in range(PIECE // STATE):
             cols = pl.ds(pl.multiple_of(p * PIECE + c * STATE, STATE), STATE)
-            skip_row = jnp.where(first_half, skip[p * PER + 2 * c], skip[p * PER + 2 * c + 1])
             for r in range(0, BLOCK, STRIP):
                 a, b = conv(r, cols)
-                here = (p, pl.ds(r, STRIP), pl.ds(c * STATE, STATE))
-                va[here] = a
-                vb[here] = b
-                acc[here] = skip_row * a.astype(F32)
-        wide = dot(aft[v], sel[q, :, 0 : 2 * PIECE])
-        wf = (va[p].astype(F32) * wide[:, :PIECE]).astype(BF16)
-        stf[p] = dot(kt[0], wf)
-        wr = (vb[p].astype(F32) * wide[:, PIECE:]).astype(BF16)
-        str_[p] = dot(kt[1], wr)
+                at = (r + half) % BLOCK
+                vcat[p, pl.ds(at, STRIP), pl.ds(c * STATE, STATE)] = a
+                vcat[p, pl.ds(BLOCK + at, STRIP), pl.ds(c * STATE, STATE)] = b
         ends = dot(aft[v, BLOCK - 16 : BLOCK, :], sel[q, :, 2 * PIECE : 3 * PIECE])
         drow[p, 0:1, :] = ends[15:16, :]
+        for i, (st, sb, first, gives) in enumerate(
+            (
+                (stf, sbf, jnp.logical_not(has_left), has_right),
+                (str_, sbr, jnp.logical_not(has_right), has_left),
+            )
+        ):
+            wide = dot(aft[v], sel[q, :, i * PIECE : (i + 1) * PIECE])
+            top = i * BLOCK
+            w = jnp.concatenate(
+                [
+                    (vcat[p, top : top + half, :].astype(F32) * wide[hi]).astype(BF16),
+                    (vcat[p, top + half : top + BLOCK, :].astype(F32) * wide[lo]).astype(BF16),
+                ],
+                axis=0,
+            )
+            state = dot(kt[i], w)
+            st[p] = state
+
+            @pl.when(first)
+            def _():
+                sb[p] = state.astype(BF16)
+                hop(p, i == 0)[0].start()
 
     def hop(p, forward):
         cin, sb, st = (cinf, sbf, stf) if forward else (cinr, sbr, str_)
@@ -222,7 +241,7 @@
         )
         return copy, cin, sb, st, takes, gives
 
-    def chain(p, forward):
+    def relay(p, forward):
         copy, cin, sb, st, takes, gives = hop(p, forward)
 
         @pl.when(takes)
@@ -232,111 +251,91 @@
             @pl.when(gives)
             def _():
                 sb[p] = (st[p] + drow[p, 0:1, :] * cin[p].astype(F32)).astype(BF16)
-
-        @pl.when(jnp.logical_not(takes))
-        def _():
-            sb[p] = st[p].astype(BF16)
-
-        @pl.when(gives)
-        def _():
-            copy.start()
+                copy.start()
+
+    def enter(p, forward):
+        cin, acc = (cinf, accf) if forward else (cinr, accr)
+        takes = has_left if forward else has_right
 
         @pl.when(takes)
         def _():
             first = (2 if forward else 3) * PIECE
             grow = dot(aft[p // 4], sel[lax.rem(p, 4), :, first : first + PIECE])
-            acc[p] = acc[p] + grow * dot(kq[1 if forward else 3], cin[p])
-
-    half = BLOCK // 2
+            acc[p] = grow * dot(kq[1 if forward else 3], cin[p])
+
+        @pl.when(jnp.logical_not(takes))
+        def _():
+            acc[p] = jnp.zeros((BLOCK, PIECE), F32)
 
     def within(p):
         for pair in range(PER // 2):
             lanes = slice(pair * STATE, (pair + 1) * STATE)
-            vf = va[p, :, lanes]
-            vr = vb[p, :, lanes]
-            res = []
+            tops, lows = [], []
             for j in (2 * pair, 2 * pair + 1):
                 cft = colc[p, :, j : j + 1]
                 cet = colc[p, :, 64 + j : 65 + j]
                 ra = rowc[p, j : j + 1, :]
                 rb = rowc[p, PER + j : PER + j + 1, :]
-                lo, hi = slice(0, half), slice(half, BLOCK)
                 d00 = jnp.exp2(jnp.minimum(cft[lo] - ra[:, lo], rb[:, lo] - cet[lo]))
-                d01 = jnp.exp2(rb[:, hi] - cet[lo])
                 f00 = (gf_ref[lo, lo] * d00).astype(BF16)
                 r00 = (gr_ref[lo, lo] * d00).astype(BF16)
+                d01 = jnp.exp2(rb[:, hi] - cet[lo])
                 r01 = (gr_ref[lo, hi] * d01).astype(BF16)
-                top = dot(f00, vf[lo]) + dot(jnp.concatenate([r00, r01], axis=1), vr)
+                tops.append(jnp.concatenate([f00, r01, r00], axis=1))
                 d11 = jnp.exp2(jnp.minimum(cft[hi] - ra[:, hi], rb[:, hi] - cet[hi]))
+                f11 = (gf_ref[hi, hi] * d11).astype(BF16)
+                r11 = (gr_ref[hi, hi] * d11).astype(BF16)
                 d10 = jnp.exp2(cft[hi] - ra[:, lo])
                 f10 = (gf_ref[hi, lo] * d10).astype(BF16)
-                f11 = (gf_ref[hi, hi] * d11).astype(BF16)
-                r11 = (gr_ref[hi, hi] * d11).astype(BF16)
-                low = dot(jnp.concatenate([f10, f11], axis=1), vf) + dot(r11, vr[hi])
-                res.append((top, low))
-            for i, rows in enumerate((slice(0, half), slice(half, BLOCK))):
-                acc[p, rows, lanes] = acc[p, rows, lanes] + jnp.where(
-                    first_half, res[0][i], res[1][i]
-                )
-        for r in range(0, BLOCK, STRIP):
-            g = gate_v[r : r + STRIP, pl.ds(pl.multiple_of(p * PIECE, PIECE), PIECE)]
-            sg[p, r : r + STRIP, :] = silu(g.astype(F32))
-
-    def slot(k, carry):
-        kf = k - LAG * me
-        kr = k - LAG * (n - 1 - me)
-        kw = k - PIECES
-
-        @pl.when(k < PIECES)
-        def _():
-            make(k)
-
-        @pl.when(jnp.logical_and(kf >= 0, kf < PIECES))
-        def _():
-            chain(kf, True)
-
-        @pl.when(jnp.logical_and(kr >= 0, kr < PIECES))
-        def _():
-            chain(kr, False)
-
-        @pl.when(jnp.logical_and(kw >= 0, kw < PIECES))
-        def _():
-            within(kw)
-
-        return carry
-
-    lax.fori_loop(0, PIECES + max(LAG * (n - 1), PIECES), slot, 0)
-
-    ssq[...] = jnp.zeros_like(ssq)
-
-    def gather(p, carry):
+                lows.append(jnp.concatenate([f11, f10, r11], axis=1))
+            top = dot(jnp.concatenate(tops, axis=0), vcat[p, half : 2 * BLOCK, lanes])
+            low = dot(jnp.concatenate(lows, axis=0), vcat[p, 0 : BLOCK + half, lanes])
+            skip_row = jnp.where(first_half, skip[p * PER + 2 * pair], skip[p * PER + 2 * pair + 1])
+            for rows, res, at in ((lo, top, half), (hi, low, 0)):
+                direct = skip_row * vcat[p, at : at + half, lanes].astype(F32)
+                accw[p, rows, lanes] = direct + jnp.where(first_half, res[:half], res[half:])
+
+    def y_copy(p):
+        cols = pl.ds(pl.multiple_of(p * PIECE, PIECE), PIECE)
+        return pltpu.make_async_copy(y_v.at[p], y_hbm.at[:, cols], out_sem.at[p])
+
+    def gather(p):
+        cols = pl.ds(pl.multiple_of(p * PIECE, PIECE), PIECE)
         for r in range(0, BLOCK, STRIP):
             rows = pl.ds(r, STRIP)
-            y = acc[p, rows, :] * sg[p, rows, :]
-            acc[p, rows, :] = y
+            gate = silu(gate_v[rows, cols].astype(F32))
+            y = (accw[p, rows, :] + (accf[p, rows, :] + accr[p, rows, :])) * gate
+            y_v[p, rows, :] = y.astype(BF16)
             y = y * y
             ssq[rows, :] = ssq[rows, :] + (y[:, :STATE] + y[:, STATE:])
+        y_copy(p).start()
+
+    ssq[...] = jnp.zeros_like(ssq)
+    behind_f = LAG * me
+    behind_r = LAG * (n - 1 - me)
+    behind_w = PIECES
+    behind_y = jnp.maximum(jnp.maximum(behind_f, behind_r), behind_w)
+
+    def slot(k, carry):
+        def step(late, work):
+            p = k - late
+
+            @pl.when(jnp.logical_and(p >= 0, p < PIECES))
+            def _():
+                work(p)
+
+        step(behind_f, lambda p: relay(p, True))
+        step(behind_r, lambda p: relay(p, False))
+        step(0, make)
+        step(behind_w, within)
+        step(behind_f, lambda p: enter(p, True))
+        step(behind_r, lambda p: enter(p, False))
+        step(behind_y, gather)
         return carry
 
-    lax.fori_loop(0, PIECES, gather, 0)
-    scale = lax.rsqrt(jnp.sum(ssq[...], axis=1, keepdims=True) * (1.0 / INNER) + 1e-05)
-    ssq[...] = jnp.broadcast_to(scale, ssq.shape)
-
-    copies = []
-    for i, r in enumerate(range(0, BLOCK, STRIP)):
-        rows = pl.ds(r, STRIP)
-
-        def emit(p, carry):
-            cols = pl.ds(pl.multiple_of(p * PIECE, PIECE), PIECE)
-            s = ssq[rows, :]
-            s = jnp.concatenate([s, s], axis=1)
-            out_v[rows, cols] = (acc[p, rows, :] * s * gain[:, cols]).astype(BF16)
-            return carry
-
-        lax.fori_loop(0, PIECES, emit, 0)
-        copy = pltpu.make_async_copy(out_v.at[rows], out_hbm.at[rows], out_sem.at[i])
-        copy.start()
-        copies.append(copy)
+    lax.fori_loop(0, PIECES + max(LAG * (n - 1), PIECES), slot, 0)
+    mean = jnp.sum(ssq[...], axis=1, keepdims=True) * (1.0 / INNER)
+    scale_ref[...] = jnp.broadcast_to(lax.rsqrt(mean + 1e-05), scale_ref.shape)
 
     @pl.when(has_right)
     def _():
@@ -354,8 +353,11 @@
 
         lax.fori_loop(0, PIECES, done, 0)
 
-    for copy in copies:
-        copy.wait()
+    def stored(p, carry):
+        y_copy(p).wait()
+        return carry
+
+    lax.fori_loop(0, PIECES, stored, 0)
 
 
 def per_device(
@@ -368,16 +370,19 @@
     piece = (PIECES, BLOCK, PIECE)
     state = (PIECES, STATE, PIECE)
     dma = pltpu.SemaphoreType.DMA
-    return pl.pallas_call(
+    y, scale = pl.pallas_call(
         functools.partial(kernel, n),
-        out_shape=jax.ShapeDtypeStruct((BLOCK, INNER), BF16),
-        in_specs=[hbm, hbm, vmem, vmem, vmem, smem, smem, vmem],
-        out_specs=hbm,
+        out_shape=(
+            jax.ShapeDtypeStruct((BLOCK, INNER), BF16),
+            jax.ShapeDtypeStruct((BLOCK, STATE), F32),
+        ),
+        in_specs=[hbm, hbm, vmem, vmem, vmem, smem, smem],
+        out_specs=(hbm, vmem),
         scratch_shapes=[
             pltpu.VMEM((BLOCK + 2 * HALO, INNER + 2 * STATE), BF16),
             pltpu.VMEM((BLOCK, INNER), BF16),
-            pltpu.VMEM(piece, BF16),
-            pltpu.VMEM(piece, BF16),
+            pltpu.VMEM((PIECES, 2 * BLOCK, PIECE), BF16),
+            pltpu.VMEM(piece, F32),
             pltpu.VMEM(piece, F32),
             pltpu.VMEM(piece, F32),
             pltpu.VMEM(state, F32),
@@ -398,7 +403,7 @@
             pltpu.VMEM((4, BLOCK, STATE), BF16),
             pltpu.VMEM((2, STATE, BLOCK), BF16),
             pltpu.VMEM((BLOCK, STATE), F32),
-            pltpu.VMEM((BLOCK, INNER), BF16),
+            pltpu.VMEM(piece, BF16),
             dma((2,)),
             dma((2,)),
             dma((2,)),
@@ -406,7 +411,7 @@
             dma((PIECES,)),
             dma((PIECES,)),
             dma((PIECES,)),
-            dma((BLOCK // STRIP,)),
+            dma((PIECES,)),
         ],
         compiler_params=pltpu.CompilerParams(
             collective_id=0, has_side_effects=True, vmem_limit_bytes=56 * 1024 * 1024
@@ -414,9 +419,9 @@
         cost_estimate=pl.CostEstimate(flops=3 * 10**9, bytes_accessed=7 * 10**6, transcendentals=10**7),
         name="mixer",
     )(
-        mixer_input, gate_input, conv_forward, conv_reverse, step_size, decay_rate, skip_scale,
-        norm_gain.reshape(1, INNER),
-    )
+        mixer_input, gate_input, conv_forward, conv_reverse, step_size, decay_rate, skip_scale
+    )
+    return (y.astype(F32) * scale[:, :1] * norm_gain).astype(BF16)
 
 
 def solution(mesh):

time: 52.6 us -> 56 us (1.065)
  other arithmetic: 0 us -> 3.54 us
  local copies, waits for them, and re-layouts: 3.13 us -> 1.01 us
  Pallas kernels: 49.3 us -> 51.3 us
    convert_element_type x0 -> x1, other arithmetic: none -> 3.54 us  [per_device(): return (y.astype(F32) * scale[:, :1] * norm_gain).astype(BF16)]
    unnamed x1 -> x2, local copies, waits for them, and re-layouts: 3.13 us -> 0.01 us
    pallas_call x1, Pallas kernels: 49.3 us -> 51.3 us  [per_device(): pl.pallas_call(functools.partial(kernel, n), out_shape=(jax.ShapeDtypeStr...]
    slice x0 -> x1, local copies, waits for them, and re-layouts: none -> 1.01 us  [per_device(): return (y.astype(F32) * scale[:, :1] * norm_gain).astype(BF16)]
where the time goes in v2:
time: 56 us; the launch traced here: 55.8 us
  Pallas kernels  51.3 us (92%)
  other arithmetic  3.54 us (6%)
  local copies, waits for them, and re-layouts  1.01 us (2%)
    pallas_call x1, Pallas kernels, per_device(): pl.pallas_call(functools.partial(kernel, n), out_shape=(jax.ShapeDtypeStr...  51.3 us
    convert_element_type x1, other arithmetic, per_device(): return (y.astype(F32) * scale[:, :1] * norm_gain).astype(BF16)  3.54 us

profile of v2, /device:TPU:0, one launch (start us, length us, event | category | flops | bytes accessed | tf_op | source)
XLA Modules:
  0.0 55.8 jit_solution(656112871210807961)
XLA Ops:
  0.0 0.0 copy-start
  0.0 51.3 %mixer.1 = (bf16[256,4096]{1,0:T(8,128)(2,1)}, f32[256,128]{1,0:T(8,128)}) custom-call(bf16[256,4352]{1,0:T(8,128)(2,1)} %x_hbm.1, bf16[256,4096]{1,0:T(8,128)(2,1)} %gate_hbm.1, f32[4,4352]{1,0:T(4,128)} %tapf.1, f32[4,4352]{1,0:T(4,128)} %tapr.1, f32[64,256]{1,0:T(8,128)} %step_ref.1, f32[64]{0:T(128)} %decay.1, f32[64]{0:T(128)} %skip.1), custom_call_target="tpu_custom_call" | custom-call | flops 3000000000 | bytes 7000000 | tf_op jit(solution)/shard_map/mixer/pallas_call | solution.py:373
  51.3 1.0 %slice_reduce_fusion = f32[256]{0:T(256)S(1)} fusion(f32[256,128]{1,0:T(8,128)} %get-tuple-element.8), kind=kLoop, calls=%fused_computation.1 | loop fusion | bytes 2048 | tf_op jit(solution)/shard_map/slice | solution.py:424
  52.3 0.0 copy-done
  52.3 3.5 %multiply_convert_fusion = bf16[256,4096]{1,0:T(8,128)(2,1)} fusion(bf16[256,4096]{1,0:T(8,128)(2,1)} %get-tuple-element.7, f32[4096]{0:T(1024)S(1)} %copy-done, f32[256]{0:T(256)S(1)} %slice_reduce_fusion), kind=kLoop, calls=%fused_computation | loop fusion | flops 4194304 | bytes 4211712 | tf_op jit(solution)/shard_map/convert_element_type | solution.py:424
Async XLA Ops:
  0.0 52.3 %copy-start = (f32[4096]{0:T(1024)S(1)}, f32[4096]{0:T(1024)}, u32[]{:S(2)}) copy-start(f32[4096]{0:T(1024)} %param.15) | copy-start | bytes 49156

commit v3 on v2

--- a/solution.py
+++ b/solution.py
@@ -18,7 +18,7 @@
 PER = PIECE // HEAD_DIM
 HALO = 16
 STRIP = 64
-LAG = 4
+LAG = 2
 LOG2E = 1.4426950408889634
 F32 = jnp.float32
 BF16 = jnp.bfloat16
@@ -37,7 +37,7 @@
 def kernel(
     n,
     x_hbm, gate_hbm, tapf, tapr, step_ref, decay, skip, y_hbm, scale_ref,
-    xpad, gate_v, vcat, accw, accf, accr, stf, str_, cinf, cinr, sbf, sbr,
+    xpad, gate_v, vcat, accw, stf, str_, cinf, cinr, sbf, sbr,
     colc, cfs, ces, rowc, aft, sel, drow, gf_ref, gr_ref, kq, kt, ssq, y_v,
     local_sem, halo_send, halo_recv, sendf, recvf, sendr, recvr, out_sem,
 ):
@@ -91,10 +91,12 @@
 
     @pl.when(jnp.logical_not(has_left))
     def _():
+        cinf[...] = jnp.zeros(cinf.shape, BF16)
         xpad[0:HALO, :] = jnp.zeros((HALO, xpad.shape[1]), BF16)
 
     @pl.when(jnp.logical_not(has_right))
     def _():
+        cinr[...] = jnp.zeros(cinr.shape, BF16)
         xpad[HALO + BLOCK :, :] = jnp.zeros((HALO, xpad.shape[1]), BF16)
 
     for h in range(HEADS):
@@ -191,9 +193,7 @@
     lane = lax.broadcasted_iota(jnp.int32, (1, STATE), 1)
     first_half = lane < HEAD_DIM
 
-    def make(p):
-        v = p // 4
-        q = lax.rem(p, 4)
+    def convolve(p):
         for c in range(PIECE // STATE):
             cols = pl.ds(pl.multiple_of(p * PIECE + c * STATE, STATE), STATE)
             for r in range(0, BLOCK, STRIP):
@@ -201,14 +201,13 @@
                 at = (r + half) % BLOCK
                 vcat[p, pl.ds(at, STRIP), pl.ds(c * STATE, STATE)] = a
                 vcat[p, pl.ds(BLOCK + at, STRIP), pl.ds(c * STATE, STATE)] = b
+
+    def states(p):
+        v = p // 4
+        q = lax.rem(p, 4)
         ends = dot(aft[v, BLOCK - 16 : BLOCK, :], sel[q, :, 2 * PIECE : 3 * PIECE])
         drow[p, 0:1, :] = ends[15:16, :]
-        for i, (st, sb, first, gives) in enumerate(
-            (
-                (stf, sbf, jnp.logical_not(has_left), has_right),
-                (str_, sbr, jnp.logical_not(has_right), has_left),
-            )
-        ):
+        for i, st in enumerate((stf, str_)):
             wide = dot(aft[v], sel[q, :, i * PIECE : (i + 1) * PIECE])
             top = i * BLOCK
             w = jnp.concatenate(
@@ -218,54 +217,33 @@
                 ],
                 axis=0,
             )
-            state = dot(kt[i], w)
-            st[p] = state
-
-            @pl.when(first)
-            def _():
-                sb[p] = state.astype(BF16)
-                hop(p, i == 0)[0].start()
+            st[p] = dot(kt[i], w)
 
     def hop(p, forward):
-        cin, sb, st = (cinf, sbf, stf) if forward else (cinr, sbr, str_)
+        sb, cin = (sbf, cinf) if forward else (sbr, cinr)
         send, recv = (sendf, recvf) if forward else (sendr, recvr)
-        takes, gives = (has_left, has_right) if forward else (has_right, has_left)
-        target = right if forward else left
-        copy = pltpu.make_async_remote_copy(
+        return pltpu.make_async_remote_copy(
             src_ref=sb.at[p],
             dst_ref=cin.at[p],
             send_sem=send.at[p],
             recv_sem=recv.at[p],
-            device_id={"seq": target},
+            device_id={"seq": right if forward else left},
             device_id_type=MESH,
         )
-        return copy, cin, sb, st, takes, gives
 
     def relay(p, forward):
-        copy, cin, sb, st, takes, gives = hop(p, forward)
+        copy = hop(p, forward)
+        cin, sb, st = (cinf, sbf, stf) if forward else (cinr, sbr, str_)
+        takes, gives = (has_left, has_right) if forward else (has_right, has_left)
 
         @pl.when(takes)
         def _():
             copy.wait_recv()
 
-            @pl.when(gives)
-            def _():
-                sb[p] = (st[p] + drow[p, 0:1, :] * cin[p].astype(F32)).astype(BF16)
-                copy.start()
-
-    def enter(p, forward):
-        cin, acc = (cinf, accf) if forward else (cinr, accr)
-        takes = has_left if forward else has_right
-
-        @pl.when(takes)
+        @pl.when(gives)
         def _():
-            first = (2 if forward else 3) * PIECE
-            grow = dot(aft[p // 4], sel[lax.rem(p, 4), :, first : first + PIECE])
-            acc[p] = grow * dot(kq[1 if forward else 3], cin[p])
-
-        @pl.when(jnp.logical_not(takes))
-        def _():
-            acc[p] = jnp.zeros((BLOCK, PIECE), F32)
+            sb[p] = (st[p] + drow[p, 0:1, :] * cin[p].astype(F32)).astype(BF16)
+            copy.start()
 
     def within(p):
         for pair in range(PER // 2):
@@ -299,48 +277,66 @@
         cols = pl.ds(pl.multiple_of(p * PIECE, PIECE), PIECE)
         return pltpu.make_async_copy(y_v.at[p], y_hbm.at[:, cols], out_sem.at[p])
 
-    def gather(p):
+    def finish(p):
+        v = p // 4
+        q = lax.rem(p, 4)
         cols = pl.ds(pl.multiple_of(p * PIECE, PIECE), PIECE)
-        for r in range(0, BLOCK, STRIP):
-            rows = pl.ds(r, STRIP)
-            gate = silu(gate_v[rows, cols].astype(F32))
-            y = (accw[p, rows, :] + (accf[p, rows, :] + accr[p, rows, :])) * gate
-            y_v[p, rows, :] = y.astype(BF16)
-            y = y * y
-            ssq[rows, :] = ssq[rows, :] + (y[:, :STATE] + y[:, STATE:])
+        growf = dot(aft[v], sel[q, :, 2 * PIECE : 3 * PIECE])
+        growr = dot(aft[v], sel[q, :, 3 * PIECE : 4 * PIECE])
+        f = dot(kq[1], cinf[p])
+        r = dot(kq[3], cinr[p])
+        gate = silu(gate_v[:, cols].astype(F32))
+        y = (accw[p] + (growf * f + growr * r)) * gate
+        y_v[p] = y.astype(BF16)
+        y = y * y
+        ssq[...] = ssq[...] + (y[:, :STATE] + y[:, STATE:])
         y_copy(p).start()
 
     ssq[...] = jnp.zeros_like(ssq)
-    behind_f = LAG * me
-    behind_r = LAG * (n - 1 - me)
-    behind_w = PIECES
-    behind_y = jnp.maximum(jnp.maximum(behind_f, behind_r), behind_w)
-
-    def slot(k, carry):
-        def step(late, work):
+    second = 1 + max(PIECES, LAG * (n - 1))
+
+    def relays(k):
+        for forward, late in ((True, 1 + LAG * me), (False, 1 + LAG * (n - 1 - me))):
             p = k - late
 
             @pl.when(jnp.logical_and(p >= 0, p < PIECES))
             def _():
-                work(p)
-
-        step(behind_f, lambda p: relay(p, True))
-        step(behind_r, lambda p: relay(p, False))
-        step(0, make)
-        step(behind_w, within)
-        step(behind_f, lambda p: enter(p, True))
-        step(behind_r, lambda p: enter(p, False))
-        step(behind_y, gather)
+                relay(p, forward)
+
+    convolve(0)
+
+    def slot_a(k, carry):
+        states(k - 1)
+        convolve(k)
+        relays(k)
         return carry
 
-    lax.fori_loop(0, PIECES + max(LAG * (n - 1), PIECES), slot, 0)
+    lax.fori_loop(1, PIECES, slot_a, 0)
+    states(PIECES - 1)
+
+    def slot_idle(k, carry):
+        relays(k)
+        return carry
+
+    lax.fori_loop(PIECES, second, slot_idle, 0)
+    relays(second)
+    within(0)
+
+    def slot_b(k, carry):
+        relays(k)
+        finish(k - second - 1)
+        within(k - second)
+        return carry
+
+    lax.fori_loop(second + 1, second + PIECES, slot_b, 0)
+    finish(PIECES - 1)
     mean = jnp.sum(ssq[...], axis=1, keepdims=True) * (1.0 / INNER)
     scale_ref[...] = jnp.broadcast_to(lax.rsqrt(mean + 1e-05), scale_ref.shape)
 
     @pl.when(has_right)
     def _():
         def done(p, carry):
-            hop(p, True)[0].wait_send()
+            hop(p, True).wait_send()
             return carry
 
         lax.fori_loop(0, PIECES, done, 0)
@@ -348,7 +344,7 @@
     @pl.when(has_left)
     def _():
         def done(p, carry):
-            hop(p, False)[0].wait_send()
+            hop(p, False).wait_send()
             return carry
 
         lax.fori_loop(0, PIECES, done, 0)
@@ -358,6 +354,25 @@
         return carry
 
     lax.fori_loop(0, PIECES, stored, 0)
+
+
+def scale_rows(y_hbm, scale_ref, gain_ref, out_hbm, y_v, out_v, in_sem, out_sem):
+    parts = [pl.ds(r, STRIP) for r in range(0, BLOCK, STRIP)]
+    loads = [pltpu.make_async_copy(y_hbm.at[s], y_v.at[s], in_sem.at[i]) for i, s in enumerate(parts)]
+    stores = [
+        pltpu.make_async_copy(out_v.at[s], out_hbm.at[s], out_sem.at[i]) for i, s in enumerate(parts)
+    ]
+    for load in loads:
+        load.start()
+    for i, rows in enumerate(parts):
+        loads[i].wait()
+        scale = scale_ref[rows, :]
+        for c in range(0, INNER, STATE):
+            cols = pl.ds(c, STATE)
+            out_v[rows, cols] = (y_v[rows, cols].astype(F32) * scale * gain_ref[:, cols]).astype(BF16)
+        stores[i].start()
+    for store in stores:
+        store.wait()
 
 
 def per_device(
@@ -382,8 +397,6 @@
             pltpu.VMEM((BLOCK + 2 * HALO, INNER + 2 * STATE), BF16),
             pltpu.VMEM((BLOCK, INNER), BF16),
             pltpu.VMEM((PIECES, 2 * BLOCK, PIECE), BF16),
-            pltpu.VMEM(piece, F32),
-            pltpu.VMEM(piece, F32),
             pltpu.VMEM(piece, F32),
             pltpu.VMEM(state, F32),
             pltpu.VMEM(state, F32),
@@ -421,7 +434,23 @@
     )(
         mixer_input, gate_input, conv_forward, conv_reverse, step_size, decay_rate, skip_scale
     )
-    return (y.astype(F32) * scale[:, :1] * norm_gain).astype(BF16)
+    dma = pltpu.SemaphoreType.DMA
+    parts = BLOCK // STRIP
+    return pl.pallas_call(
+        scale_rows,
+        out_shape=jax.ShapeDtypeStruct((BLOCK, INNER), BF16),
+        in_specs=[hbm, vmem, vmem],
+        out_specs=hbm,
+        scratch_shapes=[
+            pltpu.VMEM((BLOCK, INNER), BF16),
+            pltpu.VMEM((BLOCK, INNER), BF16),
+            dma((parts,)),
+            dma((parts,)),
+        ],
+        compiler_params=pltpu.CompilerParams(vmem_limit_bytes=32 * 1024 * 1024),
+        cost_estimate=pl.CostEstimate(flops=2 * 10**6, bytes_accessed=4 * 10**6, transcendentals=0),
+        name="scale_rows",
+    )(y, scale, norm_gain.reshape(1, INNER))
 
 
 def solution(mesh):

time: 56 us -> 53.2 us (0.950)
  other arithmetic: 3.54 us -> 0 us
  local copies, waits for them, and re-layouts: 1.01 us -> 2.49 us
  Pallas kernels: 51.3 us -> 50.3 us
    convert_element_type x1 -> x0, other arithmetic: 3.54 us -> none  [per_device(): return (y.astype(F32) * scale[:, :1] * norm_gain).astype(BF16)]
    pallas_call x1, Pallas kernels: 51.3 us -> 48.7 us  [per_device(): pl.pallas_call(functools.partial(kernel, n), out_shape=(jax.ShapeDtypeStr...]
    unnamed x2 -> x6, local copies, waits for them, and re-layouts: 0.01 us -> 2.49 us
    pallas_call x0 -> x1, Pallas kernels: none -> 1.66 us  [per_device(): pl.pallas_call(scale_rows, out_shape=jax.ShapeDtypeStruct((BLOCK, INNER),...]
    slice x1 -> x0, local copies, waits for them, and re-layouts: 1.01 us -> none  [per_device(): return (y.astype(F32) * scale[:, :1] * norm_gain).astype(BF16)]
where the time goes in v3:
time: 53.2 us; the launch traced here: 52.9 us
  Pallas kernels  50.3 us (95%)
  local copies, waits for them, and re-layouts  2.49 us (5%)
    pallas_call x1, Pallas kernels, per_device(): pl.pallas_call(functools.partial(kernel, n), out_shape=(jax.ShapeDtypeStr...  48.7 us
    unnamed x6, local copies, waits for them, and re-layouts  2.49 us
    pallas_call x1, Pallas kernels, per_device(): pl.pallas_call(scale_rows, out_shape=jax.ShapeDtypeStruct((BLOCK, INNER),...  1.66 us

profile of v3, /device:TPU:0, one launch (start us, length us, event | category | flops | bytes accessed | tf_op | source)
XLA Modules:
  0.0 52.9 jit_solution(4512210630170737190)
XLA Ops:
  0.0 0.0 copy-start.2
  0.0 48.7 %mixer.1 = (bf16[256,4096]{1,0:T(8,128)(2,1)}, f32[256,128]{1,0:T(8,128)}) custom-call(bf16[256,4352]{1,0:T(8,128)(2,1)} %x_hbm.1, bf16[256,4096]{1,0:T(8,128)(2,1)} %gate_hbm.1, f32[4,4352]{1,0:T(4,128)} %tapf.1, f32[4,4352]{1,0:T(4,128)} %tapr.1, f32[64,256]{1,0:T(8,128)} %step_ref.1, f32[64]{0:T(128)} %decay.1, f32[64]{0:T(128)} %skip.1), custom_call_target="tpu_custom_call" | custom-call | flops 3000000000 | bytes 7000000 | tf_op jit(solution)/shard_map/mixer/pallas_call | solution.py:388
  48.7 0.0 copy-done.2
  48.7 0.0 copy-start
  48.7 1.6 %copy-done = bf16[256,4096]{1,0:T(8,128)(2,1)S(1)} copy-done((bf16[256,4096]{1,0:T(8,128)(2,1)S(1)}, bf16[256,4096]{1,0:T(8,128)(2,1)}, u32[]{:S(2)}) %copy-start) | copy-done | bytes 2097176
  50.3 0.0 copy-start.1
  50.3 0.9 %copy-done.1 = f32[256,128]{1,0:T(8,128)S(1)} copy-done((f32[256,128]{1,0:T(8,128)S(1)}, f32[256,128]{1,0:T(8,128)}, u32[]{:S(2)}) %copy-start.1) | copy-done | bytes 131096
  51.2 1.7 %scale_rows.1 = bf16[256,4096]{1,0:T(8,128)(2,1)} custom-call(bf16[256,4096]{1,0:T(8,128)(2,1)S(1)} %copy-done, f32[256,128]{1,0:T(8,128)S(1)} %copy-done.1, f32[1,4096]{1,0:T(1,128)S(1)} %bitcast.1), custom_call_target="tpu_custom_call" | custom-call | flops 2000000 | bytes 4000000 | tf_op jit(solution)/shard_map/scale_rows/pallas_call | solution.py:439
Async XLA Ops:
  0.0 48.7 %copy-start.2 = (f32[4096]{0:T(1024)S(1)}, f32[4096]{0:T(1024)}, u32[]{:S(2)}) copy-start(f32[4096]{0:T(1024)} %param.15) | copy-start | bytes 49156
  48.7 1.6 %copy-start = (bf16[256,4096]{1,0:T(8,128)(2,1)S(1)}, bf16[256,4096]{1,0:T(8,128)(2,1)}, u32[]{:S(2)}) copy-start(bf16[256,4096]{1,0:T(8,128)(2,1)} %get-tuple-element.7.y_hbm) | copy-start | bytes 6291460
  50.3 0.9 %copy-start.1 = (f32[256,128]{1,0:T(8,128)S(1)}, f32[256,128]{1,0:T(8,128)}, u32[]{:S(2)}) copy-start(f32[256,128]{1,0:T(8,128)} %get-tuple-element.8.scale_ref) | copy-start | bytes 393220

commit v4 on v3

--- a/solution.py
+++ b/solution.py
@@ -19,7 +19,6 @@
 HALO = 16
 STRIP = 64
 LAG = 2
-LOG2E = 1.4426950408889634
 F32 = jnp.float32
 BF16 = jnp.bfloat16
 MESH = pl.DeviceIdType.MESH
@@ -38,7 +37,7 @@
     n,
     x_hbm, gate_hbm, tapf, tapr, step_ref, decay, skip, y_hbm, scale_ref,
     xpad, gate_v, vcat, accw, stf, str_, cinf, cinr, sbf, sbr,
-    colc, cfs, ces, rowc, aft, sel, drow, gf_ref, gr_ref, kq, kt, ssq, y_v,
+    colc, cfs, ces, rowc, aft, sel, drow, gf_ref, gr_ref, kq, kt, ssq, y_v, xf0, xf1,
     local_sem, halo_send, halo_recv, sendf, recvf, sendr, recvr, out_sem,
 ):
     me = lax.axis_index("seq")
@@ -100,7 +99,7 @@
         xpad[HALO + BLOCK :, :] = jnp.zeros((HALO, xpad.shape[1]), BF16)
 
     for h in range(HEADS):
-        ces[h : h + 1, :] = step_ref[h : h + 1, :] * (decay[h] * -LOG2E)
+        ces[h : h + 1, :] = step_ref[h : h + 1, :] * (-decay[h])
     logs = ces[...]
     row_i = lax.broadcasted_iota(jnp.int32, (BLOCK, BLOCK), 0)
     col_i = lax.broadcasted_iota(jnp.int32, (BLOCK, BLOCK), 1)
@@ -109,7 +108,7 @@
     before = cum - logs
     total = cum[:, BLOCK - 1 : BLOCK]
     steps = step_ref[...]
-    log_steps = jnp.log(steps) * LOG2E
+    log_steps = jnp.log(steps)
     cfs[...] = cum - log_steps
     ces[...] = before + log_steps
     for p in range(PIECES):
@@ -120,10 +119,10 @@
         shift = (STATE - PER * p) % STATE
         colc[p] = pltpu.roll(columns, shift, axis=1) if shift else columns
     factors = (
-        steps * jnp.exp2(total - cum),
-        steps * jnp.exp2(before),
-        jnp.exp2(cum),
-        jnp.exp2(total - before),
+        steps * jnp.exp(total - cum),
+        steps * jnp.exp(before),
+        jnp.exp(cum),
+        jnp.exp(total - before),
     )
     parts = []
     for f in factors:
@@ -137,7 +136,7 @@
                 rows.append(low[8 * u : 8 * u + 8])
         aft[v] = jnp.transpose(jnp.concatenate(rows, axis=0)).astype(BF16)
     sel_row = lax.broadcasted_iota(jnp.int32, (STATE, PIECE), 0)
-    sel_col = lax.broadcasted_iota(jnp.int32, (STATE, PIECE), 1) // HEAD_DIM
+    sel_col = lax.broadcasted_iota(jnp.int32, (STATE, PIECE), 1) >> 6
     base = sel_row - sel_col
     for q in range(4):
         for f in range(4):
@@ -146,6 +145,7 @@
             sel[q, :, f * PIECE : (f + 1) * PIECE] = jnp.where(hit, 1.0, 0.0).astype(BF16)
 
     half = BLOCK // 2
+    xfs = (xf0, xf1)
     load_x.wait()
 
     @pl.when(has_right)
@@ -158,27 +158,21 @@
         to_right.wait_recv()
         to_left.wait_send()
 
-    def conv(r, cols):
-        xs = xpad[pl.ds(r, STRIP + 2 * HALO), cols].astype(F32)[8 : STRIP + 24]
-        ahead = behind = None
-        rows = STRIP + 16
-
-        def at(d):
-            moved = xs if d == 0 else pltpu.roll(xs, (-d) % rows, axis=0)
-            return moved[8 : 8 + STRIP]
-
+    def conv(cols, xf):
+        xf[...] = xpad[:, cols].astype(F32)
         fw = tapf[:, cols]
         rv = tapr[:, cols]
-        for k in range(WIDTH):
-            a = fw[k : k + 1] * at(k - (WIDTH - 1))
-            b = rv[k : k + 1] * at(WIDTH - 1 - k)
-            ahead = a if ahead is None else ahead + a
-            behind = b if behind is None else behind + b
-        return silu(ahead).astype(BF16), silu(behind).astype(BF16)
+        for r in range(0, BLOCK, STRIP):
+            ahead = behind = None
+            for k in range(WIDTH):
+                a = fw[k : k + 1] * xf[pl.ds(HALO + r + k - (WIDTH - 1), STRIP), :]
+                b = rv[k : k + 1] * xf[pl.ds(HALO + r + WIDTH - 1 - k, STRIP), :]
+                ahead = a if ahead is None else ahead + a
+                behind = b if behind is None else behind + b
+            yield r, silu(ahead).astype(BF16), silu(behind).astype(BF16)
 
     for which in range(2):
-        for r in range(0, BLOCK, STRIP):
-            a, b = conv(r, pl.ds(INNER + which * STATE, STATE))
+        for r, a, b in conv(pl.ds(INNER + which * STATE, STATE), xfs[which]):
             kq[which, r : r + STRIP, :] = a
             kq[2 + which, r : r + STRIP, :] = b
     lo, hi = slice(0, half), slice(half, BLOCK)
@@ -187,7 +181,7 @@
         kt[i, :, lo] = keys[:, hi]
         kt[i, :, hi] = keys[:, lo]
         inside = row_i >= col_i if i == 0 else row_i <= col_i
-        (gf_ref, gr_ref)[i][...] = jnp.where(inside, dot(kq[2 * i + 1], keys), 0.0)
+        (gf_ref, gr_ref)[i][...] = jnp.where(inside, dot(kq[2 * i + 1], keys), 0.0).astype(BF16)
     load_gate.wait()
 
     lane = lax.broadcasted_iota(jnp.int32, (1, STATE), 1)
@@ -196,8 +190,7 @@
     def convolve(p):
         for c in range(PIECE // STATE):
             cols = pl.ds(pl.multiple_of(p * PIECE + c * STATE, STATE), STATE)
-            for r in range(0, BLOCK, STRIP):
-                a, b = conv(r, cols)
+            for r, a, b in conv(cols, xfs[c]):
                 at = (r + half) % BLOCK
                 vcat[p, pl.ds(at, STRIP), pl.ds(c * STATE, STATE)] = a
                 vcat[p, pl.ds(BLOCK + at, STRIP), pl.ds(c * STATE, STATE)] = b
@@ -250,22 +243,24 @@
             lanes = slice(pair * STATE, (pair + 1) * STATE)
             tops, lows = [], []
             for j in (2 * pair, 2 * pair + 1):
-                cft = colc[p, :, j : j + 1]
-                cet = colc[p, :, 64 + j : 65 + j]
+                cft = jnp.broadcast_to(colc[p, :, j : j + 1], (BLOCK, half))
+                cet = jnp.broadcast_to(colc[p, :, 64 + j : 65 + j], (BLOCK, half))
                 ra = rowc[p, j : j + 1, :]
                 rb = rowc[p, PER + j : PER + j + 1, :]
-                d00 = jnp.exp2(jnp.minimum(cft[lo] - ra[:, lo], rb[:, lo] - cet[lo]))
-                f00 = (gf_ref[lo, lo] * d00).astype(BF16)
-                r00 = (gr_ref[lo, lo] * d00).astype(BF16)
-                d01 = jnp.exp2(rb[:, hi] - cet[lo])
-                r01 = (gr_ref[lo, hi] * d01).astype(BF16)
-                tops.append(jnp.concatenate([f00, r01, r00], axis=1))
-                d11 = jnp.exp2(jnp.minimum(cft[hi] - ra[:, hi], rb[:, hi] - cet[hi]))
-                f11 = (gf_ref[hi, hi] * d11).astype(BF16)
-                r11 = (gr_ref[hi, hi] * d11).astype(BF16)
-                d10 = jnp.exp2(cft[hi] - ra[:, lo])
-                f10 = (gf_ref[hi, lo] * d10).astype(BF16)
-                lows.append(jnp.concatenate([f11, f10, r11], axis=1))
+                d00 = jnp.exp(jnp.minimum(cft[lo] - ra[:, lo], rb[:, lo] - cet[lo])).astype(BF16)
+                d01 = jnp.exp(rb[:, hi] - cet[lo]).astype(BF16)
+                tops.append(
+                    jnp.concatenate(
+                        [gf_ref[lo, lo] * d00, gr_ref[lo, hi] * d01, gr_ref[lo, lo] * d00], axis=1
+                    )
+                )
+                d11 = jnp.exp(jnp.minimum(cft[hi] - ra[:, hi], rb[:, hi] - cet[hi])).astype(BF16)
+                d10 = jnp.exp(cft[hi] - ra[:, lo]).astype(BF16)
+                lows.append(
+                    jnp.concatenate(
+                        [gf_ref[hi, hi] * d11, gf_ref[hi, lo] * d10, gr_ref[hi, hi] * d11], axis=1
+                    )
+                )
             top = dot(jnp.concatenate(tops, axis=0), vcat[p, half : 2 * BLOCK, lanes])
             low = dot(jnp.concatenate(lows, axis=0), vcat[p, 0 : BLOCK + half, lanes])
             skip_row = jnp.where(first_half, skip[p * PER + 2 * pair], skip[p * PER + 2 * pair + 1])
@@ -411,12 +406,14 @@
             pltpu.VMEM((PIECES // 4, BLOCK, STATE), BF16),
             pltpu.VMEM((4, STATE, 4 * PIECE), BF16),
             pltpu.VMEM((PIECES, 8, PIECE), F32),
-            pltpu.VMEM((BLOCK, BLOCK), F32),
-            pltpu.VMEM((BLOCK, BLOCK), F32),
+            pltpu.VMEM((BLOCK, BLOCK), BF16),
+            pltpu.VMEM((BLOCK, BLOCK), BF16),
             pltpu.VMEM((4, BLOCK, STATE), BF16),
             pltpu.VMEM((2, STATE, BLOCK), BF16),
             pltpu.VMEM((BLOCK, STATE), F32),
             pltpu.VMEM(piece, BF16),
+            pltpu.VMEM((BLOCK + 2 * HALO, STATE), F32),
+            pltpu.VMEM((BLOCK + 2 * HALO, STATE), F32),
             dma((2,)),
             dma((2,)),
             dma((2,)),
@@ -447,7 +444,7 @@
             dma((parts,)),
             dma((parts,)),
         ],
-        compiler_params=pltpu.CompilerParams(vmem_limit_bytes=32 * 1024 * 1024),
+        compiler_params=pltpu.CompilerParams(vmem_limit_bytes=60 * 1024 * 1024),
         cost_estimate=pl.CostEstimate(flops=2 * 10**6, bytes_accessed=4 * 10**6, transcendentals=0),
         name="scale_rows",
     )(y, scale, norm_gain.reshape(1, INNER))

time: 53.2 us -> 52.2 us (0.981)
  local copies, waits for them, and re-layouts: 2.49 us -> 0 us
  Pallas kernels: 50.3 us -> 51.7 us
    unnamed x6 -> x0, local copies, waits for them, and re-layouts: 2.49 us -> none
    pallas_call x1, Pallas kernels: 1.66 us -> 3.47 us  [per_device(): pl.pallas_call(scale_rows, out_shape=jax.ShapeDtypeStruct((BLOCK, INNER),...]
where the time goes in v4:
time: 52.2 us; the launch traced here: 51.8 us
  Pallas kernels  51.7 us (99%)
    pallas_call x1, Pallas kernels, per_device(): pl.pallas_call(functools.partial(kernel, n), out_shape=(jax.ShapeDtypeStr...  48.3 us
    pallas_call x1, Pallas kernels, per_device(): pl.pallas_call(scale_rows, out_shape=jax.ShapeDtypeStruct((BLOCK, INNER),...  3.47 us

profile of v4, /device:TPU:0, one launch (start us, length us, event | category | flops | bytes accessed | tf_op | source)
XLA Modules:
  0.0 51.8 jit_solution(9036398636278486108)
XLA Ops:
  0.0 48.3 %mixer.1 = (bf16[256,4096]{1,0:T(8,128)(2,1)}, f32[256,128]{1,0:T(8,128)}) custom-call(bf16[256,4352]{1,0:T(8,128)(2,1)} %x_hbm.1, bf16[256,4096]{1,0:T(8,128)(2,1)} %gate_hbm.1, f32[4,4352]{1,0:T(4,128)} %tapf.1, f32[4,4352]{1,0:T(4,128)} %tapr.1, f32[64,256]{1,0:T(8,128)} %step_ref.1, f32[64]{0:T(128)} %decay.1, f32[64]{0:T(128)} %skip.1), custom_call_target="tpu_custom_call" | custom-call | flops 3000000000 | bytes 7000000 | tf_op jit(solution)/shard_map/mixer/pallas_call | solution.py:383
  48.3 3.5 %scale_rows.1 = bf16[256,4096]{1,0:T(8,128)(2,1)} custom-call(bf16[256,4096]{1,0:T(8,128)(2,1)} %get-tuple-element.7.y_hbm, f32[256,128]{1,0:T(8,128)} %get-tuple-element.8.scale_ref, f32[1,4096]{1,0:T(1,128)} %bitcast.1), custom_call_target="tpu_custom_call" | custom-call | flops 2000000 | bytes 4000000 | tf_op jit(solution)/shard_map/scale_rows/pallas_call | solution.py:436

commit v5 on v4

--- a/solution.py
+++ b/solution.py
@@ -18,7 +18,7 @@
 PER = PIECE // HEAD_DIM
 HALO = 16
 STRIP = 64
-LAG = 2
+LAG = 4
 F32 = jnp.float32
 BF16 = jnp.bfloat16
 MESH = pl.DeviceIdType.MESH
@@ -288,7 +288,7 @@
         y_copy(p).start()
 
     ssq[...] = jnp.zeros_like(ssq)
-    second = 1 + max(PIECES, LAG * (n - 1))
+    ready = jnp.maximum(PIECES + 1, 1 + LAG * jnp.maximum(me, n - 1 - me))
 
     def relays(k):
         for forward, late in ((True, 1 + LAG * me), (False, 1 + LAG * (n - 1 - me))):
@@ -309,22 +309,32 @@
     lax.fori_loop(1, PIECES, slot_a, 0)
     states(PIECES - 1)
 
-    def slot_idle(k, carry):
-        relays(k)
-        return carry
-
-    lax.fori_loop(PIECES, second, slot_idle, 0)
-    relays(second)
-    within(0)
-
     def slot_b(k, carry):
         relays(k)
-        finish(k - second - 1)
-        within(k - second)
+
+        @pl.when(k >= ready)
+        def _():
+            finish(k - ready)
+            within(k - PIECES)
+
+        @pl.when(k < ready)
+        def _():
+            within(k - PIECES)
+
         return carry
 
-    lax.fori_loop(second + 1, second + PIECES, slot_b, 0)
-    finish(PIECES - 1)
+    lax.fori_loop(PIECES, 2 * PIECES, slot_b, 0)
+
+    def slot_c(k, carry):
+        relays(k)
+
+        @pl.when(k >= ready)
+        def _():
+            finish(k - ready)
+
+        return carry
+
+    lax.fori_loop(2 * PIECES, ready + PIECES, slot_c, 0)
     mean = jnp.sum(ssq[...], axis=1, keepdims=True) * (1.0 / INNER)
     scale_ref[...] = jnp.broadcast_to(lax.rsqrt(mean + 1e-05), scale_ref.shape)
 

time: 52.2 us -> 46.1 us (0.88)
  Pallas kernels: 51.7 us -> 45.9 us
    pallas_call x1, Pallas kernels: 48.3 us -> 42.4 us  [per_device(): pl.pallas_call(functools.partial(kernel, n), out_shape=(jax.ShapeDtypeStr...]
where the time goes in v5:
time: 46.1 us; the launch traced here: 45.9 us
  Pallas kernels  45.9 us (100%)
    pallas_call x1, Pallas kernels, per_device(): pl.pallas_call(functools.partial(kernel, n), out_shape=(jax.ShapeDtypeStr...  42.4 us
    pallas_call x1, Pallas kernels, per_device(): pl.pallas_call(scale_rows, out_shape=jax.ShapeDtypeStruct((BLOCK, INNER),...  3.47 us

profile of v5, /device:TPU:0, one launch (start us, length us, event | category | flops | bytes accessed | tf_op | source)
XLA Modules:
  0.0 45.9 jit_solution(8397043123346562153)
XLA Ops:
  0.0 42.4 %mixer.1 = (bf16[256,4096]{1,0:T(8,128)(2,1)}, f32[256,128]{1,0:T(8,128)}) custom-call(bf16[256,4352]{1,0:T(8,128)(2,1)} %x_hbm.1, bf16[256,4096]{1,0:T(8,128)(2,1)} %gate_hbm.1, f32[4,4352]{1,0:T(4,128)} %tapf.1, f32[4,4352]{1,0:T(4,128)} %tapr.1, f32[64,256]{1,0:T(8,128)} %step_ref.1, f32[64]{0:T(128)} %decay.1, f32[64]{0:T(128)} %skip.1), custom_call_target="tpu_custom_call" | custom-call | flops 3000000000 | bytes 7000000 | tf_op jit(solution)/shard_map/mixer/pallas_call | solution.py:393
  42.4 3.5 %scale_rows.1 = bf16[256,4096]{1,0:T(8,128)(2,1)} custom-call(bf16[256,4096]{1,0:T(8,128)(2,1)} %get-tuple-element.7.y_hbm, f32[256,128]{1,0:T(8,128)} %get-tuple-element.8.scale_ref, f32[1,4096]{1,0:T(1,128)} %bitcast.1), custom_call_target="tpu_custom_call" | custom-call | flops 2000000 | bytes 4000000 | tf_op jit(solution)/shard_map/scale_rows/pallas_call | solution.py:446

commit v6 on v5

--- a/solution.py
+++ b/solution.py
@@ -18,7 +18,7 @@
 PER = PIECE // HEAD_DIM
 HALO = 16
 STRIP = 64
-LAG = 4
+LAG = 3
 F32 = jnp.float32
 BF16 = jnp.bfloat16
 MESH = pl.DeviceIdType.MESH
@@ -36,7 +36,7 @@
 def kernel(
     n,
     x_hbm, gate_hbm, tapf, tapr, step_ref, decay, skip, y_hbm, scale_ref,
-    xpad, gate_v, vcat, accw, stf, str_, cinf, cinr, sbf, sbr,
+    xpad, gate_v, vcat, accw, stf, str_, midf, midr, cinf, cinr, sbf, sbr,
     colc, cfs, ces, rowc, aft, sel, drow, gf_ref, gr_ref, kq, kt, ssq, y_v, xf0, xf1,
     local_sem, halo_send, halo_recv, sendf, recvf, sendr, recvr, out_sem,
 ):
@@ -98,6 +98,8 @@
         cinr[...] = jnp.zeros(cinr.shape, BF16)
         xpad[HALO + BLOCK :, :] = jnp.zeros((HALO, xpad.shape[1]), BF16)
 
+    half = BLOCK // 2
+    lo, hi = slice(0, half), slice(half, BLOCK)
     for h in range(HEADS):
         ces[h : h + 1, :] = step_ref[h : h + 1, :] * (-decay[h])
     logs = ces[...]
@@ -118,11 +120,15 @@
     for p in range(PIECES):
         shift = (STATE - PER * p) % STATE
         colc[p] = pltpu.roll(columns, shift, axis=1) if shift else columns
+    middle = cum[:, half - 1 : half]
+    early = lax.broadcasted_iota(jnp.int32, cum.shape, 1) < half
+    start = jnp.where(early, 0.0, middle)
+    end = jnp.where(early, middle, total)
     factors = (
-        steps * jnp.exp(total - cum),
-        steps * jnp.exp(before),
-        jnp.exp(cum),
-        jnp.exp(total - before),
+        steps * jnp.exp(end - cum),
+        steps * jnp.exp(before - start),
+        jnp.exp(cum - start),
+        jnp.exp(end - before),
     )
     parts = []
     for f in factors:
@@ -144,7 +150,6 @@
             hit = jnp.logical_or(base == off, base == off + 8)
             sel[q, :, f * PIECE : (f + 1) * PIECE] = jnp.where(hit, 1.0, 0.0).astype(BF16)
 
-    half = BLOCK // 2
     xfs = (xf0, xf1)
     load_x.wait()
 
@@ -175,11 +180,9 @@
         for r, a, b in conv(pl.ds(INNER + which * STATE, STATE), xfs[which]):
             kq[which, r : r + STRIP, :] = a
             kq[2 + which, r : r + STRIP, :] = b
-    lo, hi = slice(0, half), slice(half, BLOCK)
     for i in range(2):
         keys = jnp.transpose(kq[2 * i].astype(F32)).astype(BF16)
-        kt[i, :, lo] = keys[:, hi]
-        kt[i, :, hi] = keys[:, lo]
+        kt[i] = keys
         inside = row_i >= col_i if i == 0 else row_i <= col_i
         (gf_ref, gr_ref)[i][...] = jnp.where(inside, dot(kq[2 * i + 1], keys), 0.0).astype(BF16)
     load_gate.wait()
@@ -191,26 +194,26 @@
         for c in range(PIECE // STATE):
             cols = pl.ds(pl.multiple_of(p * PIECE + c * STATE, STATE), STATE)
             for r, a, b in conv(cols, xfs[c]):
-                at = (r + half) % BLOCK
+                at = r // half * BLOCK + r % half
                 vcat[p, pl.ds(at, STRIP), pl.ds(c * STATE, STATE)] = a
-                vcat[p, pl.ds(BLOCK + at, STRIP), pl.ds(c * STATE, STATE)] = b
+                vcat[p, pl.ds(half + at, STRIP), pl.ds(c * STATE, STATE)] = b
 
     def states(p):
         v = p // 4
         q = lax.rem(p, 4)
-        ends = dot(aft[v, BLOCK - 16 : BLOCK, :], sel[q, :, 2 * PIECE : 3 * PIECE])
-        drow[p, 0:1, :] = ends[15:16, :]
-        for i, st in enumerate((stf, str_)):
+        for i in range(2):
+            ends = dot(aft[v, i * half + half - 16 : (i + 1) * half, :], sel[q, :, 2 * PIECE : 3 * PIECE])
+            drow[p, i : i + 1, :] = ends[15:16, :]
+        for i, (st, mid) in enumerate(((stf, midf), (str_, midr))):
             wide = dot(aft[v], sel[q, :, i * PIECE : (i + 1) * PIECE])
-            top = i * BLOCK
-            w = jnp.concatenate(
-                [
-                    (vcat[p, top : top + half, :].astype(F32) * wide[hi]).astype(BF16),
-                    (vcat[p, top + half : top + BLOCK, :].astype(F32) * wide[lo]).astype(BF16),
-                ],
-                axis=0,
-            )
-            st[p] = dot(kt[i], w)
+            top = i * half
+            low = (vcat[p, top : top + half, :].astype(F32) * wide[lo]).astype(BF16)
+            high = (vcat[p, BLOCK + top : BLOCK + top + half, :].astype(F32) * wide[hi]).astype(BF16)
+            low = dot(kt[i, :, lo], low)
+            high = dot(kt[i, :, hi], high)
+            first, second = (low, high) if i == 0 else (high, low)
+            mid[p] = first
+            st[p] = second + drow[p, 1 - i : 2 - i, :] * first
 
     def hop(p, forward):
         sb, cin = (sbf, cinf) if forward else (sbr, cinr)
@@ -235,7 +238,8 @@
 
         @pl.when(gives)
         def _():
-            sb[p] = (st[p] + drow[p, 0:1, :] * cin[p].astype(F32)).astype(BF16)
+            whole = drow[p, 0:1, :] * drow[p, 1:2, :]
+            sb[p] = (st[p] + whole * cin[p].astype(F32)).astype(BF16)
             copy.start()
 
     def within(p):
@@ -247,24 +251,13 @@
                 cet = jnp.broadcast_to(colc[p, :, 64 + j : 65 + j], (BLOCK, half))
                 ra = rowc[p, j : j + 1, :]
                 rb = rowc[p, PER + j : PER + j + 1, :]
-                d00 = jnp.exp(jnp.minimum(cft[lo] - ra[:, lo], rb[:, lo] - cet[lo])).astype(BF16)
-                d01 = jnp.exp(rb[:, hi] - cet[lo]).astype(BF16)
-                tops.append(
-                    jnp.concatenate(
-                        [gf_ref[lo, lo] * d00, gr_ref[lo, hi] * d01, gr_ref[lo, lo] * d00], axis=1
-                    )
-                )
-                d11 = jnp.exp(jnp.minimum(cft[hi] - ra[:, hi], rb[:, hi] - cet[hi])).astype(BF16)
-                d10 = jnp.exp(cft[hi] - ra[:, lo]).astype(BF16)
-                lows.append(
-                    jnp.concatenate(
-                        [gf_ref[hi, hi] * d11, gf_ref[hi, lo] * d10, gr_ref[hi, hi] * d11], axis=1
-                    )
-                )
-            top = dot(jnp.concatenate(tops, axis=0), vcat[p, half : 2 * BLOCK, lanes])
-            low = dot(jnp.concatenate(lows, axis=0), vcat[p, 0 : BLOCK + half, lanes])
+                for part, rows in ((tops, lo), (lows, hi)):
+                    d = jnp.minimum(cft[rows] - ra[:, rows], rb[:, rows] - cet[rows])
+                    d = jnp.exp(d).astype(BF16)
+                    part.append(jnp.concatenate([gf_ref[rows, rows] * d, gr_ref[rows, rows] * d], axis=1))
             skip_row = jnp.where(first_half, skip[p * PER + 2 * pair], skip[p * PER + 2 * pair + 1])
-            for rows, res, at in ((lo, top, half), (hi, low, 0)):
+            for part, rows, at in ((tops, lo, 0), (lows, hi, BLOCK)):
+                res = dot(jnp.concatenate(part, axis=0), vcat[p, at : at + BLOCK, lanes])
                 direct = skip_row * vcat[p, at : at + half, lanes].astype(F32)
                 accw[p, rows, lanes] = direct + jnp.where(first_half, res[:half], res[half:])
 
@@ -278,8 +271,12 @@
         cols = pl.ds(pl.multiple_of(p * PIECE, PIECE), PIECE)
         growf = dot(aft[v], sel[q, :, 2 * PIECE : 3 * PIECE])
         growr = dot(aft[v], sel[q, :, 3 * PIECE : 4 * PIECE])
-        f = dot(kq[1], cinf[p])
-        r = dot(kq[3], cinr[p])
+        ef = cinf[p]
+        er = cinr[p]
+        late_f = (midf[p] + drow[p, 0:1, :] * ef.astype(F32)).astype(BF16)
+        late_r = (midr[p] + drow[p, 1:2, :] * er.astype(F32)).astype(BF16)
+        f = jnp.concatenate([dot(kq[1, lo, :], ef), dot(kq[1, hi, :], late_f)], axis=0)
+        r = jnp.concatenate([dot(kq[3, lo, :], late_r), dot(kq[3, hi, :], er)], axis=0)
         gate = silu(gate_v[:, cols].astype(F32))
         y = (accw[p] + (growf * f + growr * r)) * gate
         y_v[p] = y.astype(BF16)
@@ -403,6 +400,8 @@
             pltpu.VMEM((BLOCK, INNER), BF16),
             pltpu.VMEM((PIECES, 2 * BLOCK, PIECE), BF16),
             pltpu.VMEM(piece, F32),
+            pltpu.VMEM(state, F32),
+            pltpu.VMEM(state, F32),
             pltpu.VMEM(state, F32),
             pltpu.VMEM(state, F32),
             pltpu.VMEM(state, BF16),

time: 46.1 us -> 43.9 us (0.952)
  Pallas kernels: 45.9 us -> 43.7 us
    pallas_call x1, Pallas kernels: 42.4 us -> 40.2 us  [per_device(): pl.pallas_call(functools.partial(kernel, n), out_shape=(jax.ShapeDtypeStr...]
where the time goes in v6:
time: 43.9 us; the launch traced here: 43.7 us
  Pallas kernels  43.7 us (100%)
    pallas_call x1, Pallas kernels, per_device(): pl.pallas_call(functools.partial(kernel, n), out_shape=(jax.ShapeDtypeStr...  40.2 us
    pallas_call x1, Pallas kernels, per_device(): pl.pallas_call(scale_rows, out_shape=jax.ShapeDtypeStruct((BLOCK, INNER),...  3.47 us

profile of v6, /device:TPU:0, one launch (start us, length us, event | category | flops | bytes accessed | tf_op | source)
XLA Modules:
  0.0 43.7 jit_solution(16643411522202713828)
XLA Ops:
  0.0 40.2 %mixer.1 = (bf16[256,4096]{1,0:T(8,128)(2,1)}, f32[256,128]{1,0:T(8,128)}) custom-call(bf16[256,4352]{1,0:T(8,128)(2,1)} %x_hbm.1, bf16[256,4096]{1,0:T(8,128)(2,1)} %gate_hbm.1, f32[4,4352]{1,0:T(4,128)} %tapf.1, f32[4,4352]{1,0:T(4,128)} %tapr.1, f32[64,256]{1,0:T(8,128)} %step_ref.1, f32[64]{0:T(128)} %decay.1, f32[64]{0:T(128)} %skip.1), custom_call_target="tpu_custom_call" | custom-call | flops 3000000000 | bytes 7000000 | tf_op jit(solution)/shard_map/mixer/pallas_call | solution.py:390
  40.2 3.5 %scale_rows.1 = bf16[256,4096]{1,0:T(8,128)(2,1)} custom-call(bf16[256,4096]{1,0:T(8,128)(2,1)} %get-tuple-element.7.y_hbm, f32[256,128]{1,0:T(8,128)} %get-tuple-element.8.scale_ref, f32[1,4096]{1,0:T(1,128)} %bitcast.1), custom_call_target="tpu_custom_call" | custom-call | flops 2000000 | bytes 4000000 | tf_op jit(solution)/shard_map/scale_rows/pallas_call | solution.py:445

commit v7 on v6

--- a/solution.py
+++ b/solution.py
@@ -18,7 +18,8 @@
 PER = PIECE // HEAD_DIM
 HALO = 16
 STRIP = 64
-LAG = 3
+LAG = 4
+PAIR = 2
 F32 = jnp.float32
 BF16 = jnp.bfloat16
 MESH = pl.DeviceIdType.MESH
@@ -36,9 +37,10 @@
 def kernel(
     n,
     x_hbm, gate_hbm, tapf, tapr, step_ref, decay, skip, y_hbm, scale_ref,
-    xpad, gate_v, vcat, accw, stf, str_, midf, midr, cinf, cinr, sbf, sbr,
+    xpad, gate_v, vcat, accw, st, midf, midr, chain_in, peer_in, ent, give, out_sb,
     colc, cfs, ces, rowc, aft, sel, drow, gf_ref, gr_ref, kq, kt, ssq, y_v, xf0, xf1,
-    local_sem, halo_send, halo_recv, sendf, recvf, sendr, recvr, out_sem,
+    local_sem, halo_send, halo_recv,
+    peer_send, peer_recv, chain_send, chain_recv, ent_send, ent_recv, out_sem,
 ):
     me = lax.axis_index("seq")
     has_left = me > 0
@@ -53,15 +55,33 @@
 
     barrier = pltpu.get_barrier_semaphore()
 
-    @pl.when(has_left)
-    def _():
-        pl.semaphore_signal(barrier, inc=1, device_id={"seq": left}, device_id_type=MESH)
-
-    @pl.when(has_right)
-    def _():
-        pl.semaphore_signal(barrier, inc=1, device_id={"seq": right}, device_id_type=MESH)
-
-    pl.semaphore_wait(barrier, has_left.astype(jnp.int32) + has_right.astype(jnp.int32))
+    peers = jnp.int32(0)
+    for d in (-1, 1, -2, 2):
+        there = jnp.logical_and(me + d >= 0, me + d < n)
+        peers = peers + there.astype(jnp.int32)
+
+        @pl.when(there)
+        def _():
+            pl.semaphore_signal(
+                barrier, inc=1, device_id={"seq": lax.rem(me + d + n, n)}, device_id_type=MESH
+            )
+
+    pl.semaphore_wait(barrier, peers)
+
+    core = lax.rem(me, 2)
+    chip = me // 2
+    chips = n // 2
+    mine = 1 - core
+    other = core
+    far_f = chip
+    far_r = chips - 1 - chip
+    far_mine = jnp.where(core == 1, far_f, far_r)
+    far_other = jnp.where(core == 1, far_r, far_f)
+    partner = me + 1 - 2 * core
+    onward = lax.rem(me + 4 * core - 2 + n, n)
+    takes = far_mine > 0
+    gives = far_mine < chips - 1
+    fed = far_other > 0
 
     to_right = pltpu.make_async_remote_copy(
         src_ref=x_hbm.at[pl.ds(BLOCK - HALO, HALO)],
@@ -90,13 +110,19 @@
 
     @pl.when(jnp.logical_not(has_left))
     def _():
-        cinf[...] = jnp.zeros(cinf.shape, BF16)
         xpad[0:HALO, :] = jnp.zeros((HALO, xpad.shape[1]), BF16)
 
     @pl.when(jnp.logical_not(has_right))
     def _():
-        cinr[...] = jnp.zeros(cinr.shape, BF16)
         xpad[HALO + BLOCK :, :] = jnp.zeros((HALO, xpad.shape[1]), BF16)
+
+    @pl.when(jnp.logical_not(takes))
+    def _():
+        chain_in[...] = jnp.zeros(chain_in.shape, BF16)
+
+    @pl.when(jnp.logical_not(fed))
+    def _():
+        ent[other] = jnp.zeros(ent.shape[1:], BF16)
 
     half = BLOCK // 2
     lo, hi = slice(0, half), slice(half, BLOCK)
@@ -204,7 +230,7 @@
         for i in range(2):
             ends = dot(aft[v, i * half + half - 16 : (i + 1) * half, :], sel[q, :, 2 * PIECE : 3 * PIECE])
             drow[p, i : i + 1, :] = ends[15:16, :]
-        for i, (st, mid) in enumerate(((stf, midf), (str_, midr))):
+        for i, mid in enumerate((midf, midr)):
             wide = dot(aft[v], sel[q, :, i * PIECE : (i + 1) * PIECE])
             top = i * half
             low = (vcat[p, top : top + half, :].astype(F32) * wide[lo]).astype(BF16)
@@ -213,34 +239,65 @@
             high = dot(kt[i, :, hi], high)
             first, second = (low, high) if i == 0 else (high, low)
             mid[p] = first
-            st[p] = second + drow[p, 1 - i : 2 - i, :] * first
-
-    def hop(p, forward):
-        sb, cin = (sbf, cinf) if forward else (sbr, cinr)
-        send, recv = (sendf, recvf) if forward else (sendr, recvr)
+            st[i, p] = second + drow[p, 1 - i : 2 - i, :] * first
+
+        whole = drow[p, 0:1, :] * drow[p, 1:2, :]
+        high = whole.astype(BF16).astype(F32)
+        row = lax.broadcasted_iota(jnp.int32, (16, PIECE), 0)
+        tail = jnp.where(row == 0, high, jnp.where(row == 1, whole - high, 0.0))
+        give[p, 0:STATE, :] = st[other, p].astype(BF16)
+        give[p, STATE:, :] = tail.astype(BF16)
+        to_partner(p).start()
+
+    def to_partner(p):
         return pltpu.make_async_remote_copy(
-            src_ref=sb.at[p],
-            dst_ref=cin.at[p],
-            send_sem=send.at[p],
-            recv_sem=recv.at[p],
-            device_id={"seq": right if forward else left},
+            src_ref=give.at[p],
+            dst_ref=peer_in.at[p],
+            send_sem=peer_send.at[p],
+            recv_sem=peer_recv.at[p],
+            device_id={"seq": partner},
             device_id_type=MESH,
         )
 
-    def relay(p, forward):
-        copy = hop(p, forward)
-        cin, sb, st = (cinf, sbf, stf) if forward else (cinr, sbr, str_)
-        takes, gives = (has_left, has_right) if forward else (has_right, has_left)
+    def to_chip(p):
+        return pltpu.make_async_remote_copy(
+            src_ref=out_sb.at[p],
+            dst_ref=chain_in.at[p],
+            send_sem=chain_send.at[p],
+            recv_sem=chain_recv.at[p],
+            device_id={"seq": onward},
+            device_id_type=MESH,
+        )
+
+    def to_entry(p):
+        return pltpu.make_async_remote_copy(
+            src_ref=chain_in.at[p],
+            dst_ref=ent.at[mine, p],
+            send_sem=ent_send.at[p],
+            recv_sem=ent_recv.at[p],
+            device_id={"seq": partner},
+            device_id_type=MESH,
+        )
+
+    def relay(p):
+        to_partner(p).wait_recv()
 
         @pl.when(takes)
         def _():
-            copy.wait_recv()
+            to_chip(p).wait_recv()
+            to_entry(p).start()
+
+        beside = peer_in[p, STATE : STATE + 16, :].astype(F32)
+        beside = beside[0:1] + beside[1:2]
+        entry = peer_in[p, 0:STATE, :].astype(F32) + beside * chain_in[p].astype(F32)
+        whole = drow[p, 0:1, :] * drow[p, 1:2, :]
 
         @pl.when(gives)
         def _():
-            whole = drow[p, 0:1, :] * drow[p, 1:2, :]
-            sb[p] = (st[p] + whole * cin[p].astype(F32)).astype(BF16)
-            copy.start()
+            out_sb[p] = (st[mine, p] + whole * entry).astype(BF16)
+            to_chip(p).start()
+
+        ent[mine, p] = entry.astype(BF16)
 
     def within(p):
         for pair in range(PER // 2):
@@ -271,8 +328,8 @@
         cols = pl.ds(pl.multiple_of(p * PIECE, PIECE), PIECE)
         growf = dot(aft[v], sel[q, :, 2 * PIECE : 3 * PIECE])
         growr = dot(aft[v], sel[q, :, 3 * PIECE : 4 * PIECE])
-        ef = cinf[p]
-        er = cinr[p]
+        ef = ent[0, p]
+        er = ent[1, p]
         late_f = (midf[p] + drow[p, 0:1, :] * ef.astype(F32)).astype(BF16)
         late_r = (midr[p] + drow[p, 1:2, :] * er.astype(F32)).astype(BF16)
         f = jnp.concatenate([dot(kq[1, lo, :], ef), dot(kq[1, hi, :], late_f)], axis=0)
@@ -285,15 +342,17 @@
         y_copy(p).start()
 
     ssq[...] = jnp.zeros_like(ssq)
-    ready = jnp.maximum(PIECES + 1, 1 + LAG * jnp.maximum(me, n - 1 - me))
+    late = 1 + PAIR + LAG * far_mine
+    ready = jnp.maximum(jnp.maximum(PIECES + 1, late), 1 + 2 * PAIR + LAG * far_other)
 
     def relays(k):
-        for forward, late in ((True, 1 + LAG * me), (False, 1 + LAG * (n - 1 - me))):
-            p = k - late
-
-            @pl.when(jnp.logical_and(p >= 0, p < PIECES))
-            def _():
-                relay(p, forward)
+        @pl.when(jnp.logical_and(k >= late, k < late + PIECES))
+        def _():
+            relay(k - late)
+
+        @pl.when(jnp.logical_and(jnp.logical_and(k >= ready, k < ready + PIECES), fed))
+        def _():
+            to_entry(k - ready).wait_recv()
 
     convolve(0)
 
@@ -335,21 +394,20 @@
     mean = jnp.sum(ssq[...], axis=1, keepdims=True) * (1.0 / INNER)
     scale_ref[...] = jnp.broadcast_to(lax.rsqrt(mean + 1e-05), scale_ref.shape)
 
-    @pl.when(has_right)
-    def _():
-        def done(p, carry):
-            hop(p, True).wait_send()
-            return carry
-
-        lax.fori_loop(0, PIECES, done, 0)
-
-    @pl.when(has_left)
-    def _():
-        def done(p, carry):
-            hop(p, False).wait_send()
-            return carry
-
-        lax.fori_loop(0, PIECES, done, 0)
+    def done(p, carry):
+        to_partner(p).wait_send()
+
+        @pl.when(gives)
+        def _():
+            to_chip(p).wait_send()
+
+        @pl.when(takes)
+        def _():
+            to_entry(p).wait_send()
+
+        return carry
+
+    lax.fori_loop(0, PIECES, done, 0)
 
     def stored(p, carry):
         y_copy(p).wait()
@@ -400,13 +458,13 @@
             pltpu.VMEM((BLOCK, INNER), BF16),
             pltpu.VMEM((PIECES, 2 * BLOCK, PIECE), BF16),
             pltpu.VMEM(piece, F32),
-            pltpu.VMEM(state, F32),
-            pltpu.VMEM(state, F32),
+            pltpu.VMEM((2,) + state, F32),
             pltpu.VMEM(state, F32),
             pltpu.VMEM(state, F32),
             pltpu.VMEM(state, BF16),
-            pltpu.VMEM(state, BF16),
-            pltpu.VMEM(state, BF16),
+            pltpu.VMEM((PIECES, STATE + 16, PIECE), BF16),
+            pltpu.VMEM((2,) + state, BF16),
+            pltpu.VMEM((PIECES, STATE + 16, PIECE), BF16),
             pltpu.VMEM(state, BF16),
             pltpu.VMEM((PIECES, BLOCK, STATE), F32),
             pltpu.VMEM((HEADS, BLOCK), F32),
@@ -426,6 +484,8 @@
             dma((2,)),
             dma((2,)),
             dma((2,)),
+            dma((PIECES,)),
+            dma((PIECES,)),
             dma((PIECES,)),
             dma((PIECES,)),
             dma((PIECES,)),

time: 43.9 us -> 40.8 us (0.929)
  Pallas kernels: 43.7 us -> 40.6 us
    pallas_call x1, Pallas kernels: 40.2 us -> 37.1 us  [per_device(): pl.pallas_call(functools.partial(kernel, n), out_shape=(jax.ShapeDtypeStr...]
where the time goes in v7:
time: 40.8 us; the launch traced here: 40.6 us
  Pallas kernels  40.6 us (100%)
    pallas_call x1, Pallas kernels, per_device(): pl.pallas_call(functools.partial(kernel, n), out_shape=(jax.ShapeDtypeStr...  37.1 us
    pallas_call x1, Pallas kernels, per_device(): pl.pallas_call(scale_rows, out_shape=jax.ShapeDtypeStruct((BLOCK, INNER),...  3.47 us

profile of v7, /device:TPU:0, one launch (start us, length us, event | category | flops | bytes accessed | tf_op | source)
XLA Modules:
  0.0 40.6 jit_solution(565397091653533073)
XLA Ops:
  0.0 37.1 %mixer.1 = (bf16[256,4096]{1,0:T(8,128)(2,1)}, f32[256,128]{1,0:T(8,128)}) custom-call(bf16[256,4352]{1,0:T(8,128)(2,1)} %x_hbm.1, bf16[256,4096]{1,0:T(8,128)(2,1)} %gate_hbm.1, f32[4,4352]{1,0:T(4,128)} %tapf.1, f32[4,4352]{1,0:T(4,128)} %tapr.1, f32[64,256]{1,0:T(8,128)} %step_ref.1, f32[64]{0:T(128)} %decay.1, f32[64]{0:T(128)} %skip.1), custom_call_target="tpu_custom_call" | custom-call | flops 3000000000 | bytes 7000000 | tf_op jit(solution)/shard_map/mixer/pallas_call | solution.py:448
  37.1 3.5 %scale_rows.1 = bf16[256,4096]{1,0:T(8,128)(2,1)} custom-call(bf16[256,4096]{1,0:T(8,128)(2,1)} %get-tuple-element.7.y_hbm, f32[256,128]{1,0:T(8,128)} %get-tuple-element.8.scale_ref, f32[1,4096]{1,0:T(1,128)} %bitcast.1), custom_call_target="tpu_custom_call" | custom-call | flops 2000000 | bytes 4000000 | tf_op jit(solution)/shard_map/scale_rows/pallas_call | solution.py:505

commit v8 on v7

--- a/solution.py
+++ b/solution.py
@@ -19,7 +19,7 @@
 HALO = 16
 STRIP = 64
 LAG = 4
-PAIR = 2
+PAIR = 3
 F32 = jnp.float32
 BF16 = jnp.bfloat16
 MESH = pl.DeviceIdType.MESH
@@ -36,8 +36,8 @@
 
 def kernel(
     n,
-    x_hbm, gate_hbm, tapf, tapr, step_ref, decay, skip, y_hbm, scale_ref,
-    xpad, gate_v, vcat, accw, st, midf, midr, chain_in, peer_in, ent, give, out_sb,
+    x_hbm, gate_hbm, tapf_hbm, tapr_hbm, step_hbm, decay, skip, y_hbm, scale_ref,
+    tapf, tapr, step_ref, xpad, gate_v, vcat, accw, st, midf, midr, chain_in, peer_in, ent, give, out_sb,
     colc, cfs, ces, rowc, aft, sel, drow, gf_ref, gr_ref, kq, kt, ssq, y_v, xf0, xf1,
     local_sem, halo_send, halo_recv,
     peer_send, peer_recv, chain_send, chain_recv, ent_send, ent_recv, out_sem,
@@ -50,6 +50,12 @@
 
     load_x = pltpu.make_async_copy(x_hbm, xpad.at[pl.ds(HALO, BLOCK)], local_sem.at[0])
     load_gate = pltpu.make_async_copy(gate_hbm, gate_v, local_sem.at[1])
+    load_step = pltpu.make_async_copy(step_hbm, step_ref, local_sem.at[2])
+    load_tapf = pltpu.make_async_copy(tapf_hbm, tapf, local_sem.at[3])
+    load_tapr = pltpu.make_async_copy(tapr_hbm, tapr, local_sem.at[4])
+    load_step.start()
+    load_tapf.start()
+    load_tapr.start()
     load_x.start()
     load_gate.start()
 
@@ -126,6 +132,7 @@
 
     half = BLOCK // 2
     lo, hi = slice(0, half), slice(half, BLOCK)
+    load_step.wait()
     for h in range(HEADS):
         ces[h : h + 1, :] = step_ref[h : h + 1, :] * (-decay[h])
     logs = ces[...]
@@ -178,6 +185,8 @@
 
     xfs = (xf0, xf1)
     load_x.wait()
+    load_tapf.wait()
+    load_tapr.wait()
 
     @pl.when(has_right)
     def _():
@@ -451,9 +460,12 @@
             jax.ShapeDtypeStruct((BLOCK, INNER), BF16),
             jax.ShapeDtypeStruct((BLOCK, STATE), F32),
         ),
-        in_specs=[hbm, hbm, vmem, vmem, vmem, smem, smem],
+        in_specs=[hbm, hbm, hbm, hbm, hbm, smem, smem],
         out_specs=(hbm, vmem),
         scratch_shapes=[
+            pltpu.VMEM((WIDTH, INNER + 2 * STATE), F32),
+            pltpu.VMEM((WIDTH, INNER + 2 * STATE), F32),
+            pltpu.VMEM((HEADS, BLOCK), F32),
             pltpu.VMEM((BLOCK + 2 * HALO, INNER + 2 * STATE), BF16),
             pltpu.VMEM((BLOCK, INNER), BF16),
             pltpu.VMEM((PIECES, 2 * BLOCK, PIECE), BF16),
@@ -481,7 +493,7 @@
             pltpu.VMEM(piece, BF16),
             pltpu.VMEM((BLOCK + 2 * HALO, STATE), F32),
             pltpu.VMEM((BLOCK + 2 * HALO, STATE), F32),
-            dma((2,)),
+            dma((5,)),
             dma((2,)),
             dma((2,)),
             dma((PIECES,)),

time: 40.8 us -> 40.8 us (level)
  no operation moved by 1% of the time
where the time goes in v8:
time: 40.8 us; the launch traced here: 40.6 us
  Pallas kernels  40.5 us (99%)
    pallas_call x1, Pallas kernels, per_device(): pl.pallas_call(functools.partial(kernel, n), out_shape=(jax.ShapeDtypeStr...  37.1 us
    pallas_call x1, Pallas kernels, per_device(): pl.pallas_call(scale_rows, out_shape=jax.ShapeDtypeStruct((BLOCK, INNER),...  3.47 us

profile of v8, /device:TPU:0, one launch (start us, length us, event | category | flops | bytes accessed | tf_op | source)
XLA Modules:
  0.0 40.6 jit_solution(397225307532933023)
XLA Ops:
  0.0 37.1 %mixer.1 = (bf16[256,4096]{1,0:T(8,128)(2,1)}, f32[256,128]{1,0:T(8,128)}) custom-call(bf16[256,4352]{1,0:T(8,128)(2,1)} %x_hbm.1, bf16[256,4096]{1,0:T(8,128)(2,1)} %gate_hbm.1, f32[4,4352]{1,0:T(4,128)} %tapf_hbm.1, f32[4,4352]{1,0:T(4,128)} %tapr_hbm.1, f32[64,256]{1,0:T(8,128)} %step_hbm.1, f32[64]{0:T(128)} %decay.1, f32[64]{0:T(128)} %skip.1), custom_call_target="tpu_custom_call" | custom-call | flops 3000000000 | bytes 7000000 | tf_op jit(solution)/shard_map/mixer/pallas_call | solution.py:457
  37.1 3.5 %scale_rows.1 = bf16[256,4096]{1,0:T(8,128)(2,1)} custom-call(bf16[256,4096]{1,0:T(8,128)(2,1)} %get-tuple-element.7.y_hbm, f32[256,128]{1,0:T(8,128)} %get-tuple-element.8.scale_ref, f32[1,4096]{1,0:T(1,128)} %bitcast.1), custom_call_target="tpu_custom_call" | custom-call | flops 2000000 | bytes 4000000 | tf_op jit(solution)/shard_map/scale_rows/pallas_call | solution.py:517

commit v9 on v8

--- a/solution.py
+++ b/solution.py
@@ -18,6 +18,7 @@
 PER = PIECE // HEAD_DIM
 HALO = 16
 STRIP = 64
+TAIL = 32
 LAG = 4
 PAIR = 3
 F32 = jnp.float32
@@ -240,13 +241,12 @@
             ends = dot(aft[v, i * half + half - 16 : (i + 1) * half, :], sel[q, :, 2 * PIECE : 3 * PIECE])
             drow[p, i : i + 1, :] = ends[15:16, :]
         for i, mid in enumerate((midf, midr)):
-            wide = dot(aft[v], sel[q, :, i * PIECE : (i + 1) * PIECE])
-            top = i * half
-            low = (vcat[p, top : top + half, :].astype(F32) * wide[lo]).astype(BF16)
-            high = (vcat[p, BLOCK + top : BLOCK + top + half, :].astype(F32) * wide[hi]).astype(BF16)
-            low = dot(kt[i, :, lo], low)
-            high = dot(kt[i, :, hi], high)
-            first, second = (low, high) if i == 0 else (high, low)
+            parts = []
+            for at, rows in ((i * half, lo), (BLOCK + i * half, hi)):
+                wide = dot(aft[v, rows, :], sel[q, :, i * PIECE : (i + 1) * PIECE])
+                weighted = (vcat[p, at : at + half, :].astype(F32) * wide).astype(BF16)
+                parts.append(dot(kt[i, :, rows], weighted))
+            first, second = parts if i == 0 else parts[::-1]
             mid[p] = first
             st[i, p] = second + drow[p, 1 - i : 2 - i, :] * first
 
@@ -335,19 +335,20 @@
         v = p // 4
         q = lax.rem(p, 4)
         cols = pl.ds(pl.multiple_of(p * PIECE, PIECE), PIECE)
-        growf = dot(aft[v], sel[q, :, 2 * PIECE : 3 * PIECE])
-        growr = dot(aft[v], sel[q, :, 3 * PIECE : 4 * PIECE])
         ef = ent[0, p]
         er = ent[1, p]
         late_f = (midf[p] + drow[p, 0:1, :] * ef.astype(F32)).astype(BF16)
         late_r = (midr[p] + drow[p, 1:2, :] * er.astype(F32)).astype(BF16)
-        f = jnp.concatenate([dot(kq[1, lo, :], ef), dot(kq[1, hi, :], late_f)], axis=0)
-        r = jnp.concatenate([dot(kq[3, lo, :], late_r), dot(kq[3, hi, :], er)], axis=0)
-        gate = silu(gate_v[:, cols].astype(F32))
-        y = (accw[p] + (growf * f + growr * r)) * gate
-        y_v[p] = y.astype(BF16)
-        y = y * y
-        ssq[...] = ssq[...] + (y[:, :STATE] + y[:, STATE:])
+        for rows, f, r in ((lo, ef, late_r), (hi, late_f, er)):
+            y = accw[p, rows, :]
+            grow = dot(aft[v, rows, :], sel[q, :, 2 * PIECE : 3 * PIECE])
+            y = y + grow * dot(kq[1, rows, :], f)
+            grow = dot(aft[v, rows, :], sel[q, :, 3 * PIECE : 4 * PIECE])
+            y = y + grow * dot(kq[3, rows, :], r)
+            y = y * silu(gate_v[rows, cols].astype(F32))
+            y_v[p, rows, :] = y.astype(BF16)
+            y = y * y
+            ssq[rows, :] = ssq[rows, :] + (y[:, :STATE] + y[:, STATE:])
         y_copy(p).start()
 
     ssq[...] = jnp.zeros_like(ssq)
@@ -426,7 +427,7 @@
 
 
 def scale_rows(y_hbm, scale_ref, gain_ref, out_hbm, y_v, out_v, in_sem, out_sem):
-    parts = [pl.ds(r, STRIP) for r in range(0, BLOCK, STRIP)]
+    parts = [pl.ds(r, TAIL) for r in range(0, BLOCK, TAIL)]
     loads = [pltpu.make_async_copy(y_hbm.at[s], y_v.at[s], in_sem.at[i]) for i, s in enumerate(parts)]
     stores = [
         pltpu.make_async_copy(out_v.at[s], out_hbm.at[s], out_sem.at[i]) for i, s in enumerate(parts)
@@ -513,7 +514,7 @@
         mixer_input, gate_input, conv_forward, conv_reverse, step_size, decay_rate, skip_scale
     )
     dma = pltpu.SemaphoreType.DMA
-    parts = BLOCK // STRIP
+    parts = BLOCK // TAIL
     return pl.pallas_call(
         scale_rows,
         out_shape=jax.ShapeDtypeStruct((BLOCK, INNER), BF16),

time: 40.8 us -> 42.3 us (1.037)
  Pallas kernels: 40.5 us -> 42 us
    pallas_call x1, Pallas kernels: 37.1 us -> 38.6 us  [per_device(): pl.pallas_call(functools.partial(kernel, n), out_shape=(jax.ShapeDtypeStr...]
where the time goes in v9:
time: 42.3 us; the launch traced here: 42 us
  Pallas kernels  42 us (99%)
    pallas_call x1, Pallas kernels, per_device(): pl.pallas_call(functools.partial(kernel, n), out_shape=(jax.ShapeDtypeStr...  38.6 us
    pallas_call x1, Pallas kernels, per_device(): pl.pallas_call(scale_rows, out_shape=jax.ShapeDtypeStruct((BLOCK, INNER),...  3.37 us

profile of v9, /device:TPU:0, one launch (start us, length us, event | category | flops | bytes accessed | tf_op | source)
XLA Modules:
  0.0 42.0 jit_solution(9030471232866255120)
XLA Ops:
  0.0 38.6 %mixer.1 = (bf16[256,4096]{1,0:T(8,128)(2,1)}, f32[256,128]{1,0:T(8,128)}) custom-call(bf16[256,4352]{1,0:T(8,128)(2,1)} %x_hbm.1, bf16[256,4096]{1,0:T(8,128)(2,1)} %gate_hbm.1, f32[4,4352]{1,0:T(4,128)} %tapf_hbm.1, f32[4,4352]{1,0:T(4,128)} %tapr_hbm.1, f32[64,256]{1,0:T(8,128)} %step_hbm.1, f32[64]{0:T(128)} %decay.1, f32[64]{0:T(128)} %skip.1), custom_call_target="tpu_custom_call" | custom-call | flops 3000000000 | bytes 7000000 | tf_op jit(solution)/shard_map/mixer/pallas_call | solution.py:458
  38.7 3.4 %scale_rows.1 = bf16[256,4096]{1,0:T(8,128)(2,1)} custom-call(bf16[256,4096]{1,0:T(8,128)(2,1)} %get-tuple-element.7.y_hbm, f32[256,128]{1,0:T(8,128)} %get-tuple-element.8.scale_ref, f32[1,4096]{1,0:T(1,128)} %bitcast.1), custom_call_target="tpu_custom_call" | custom-call | flops 2000000 | bytes 4000000 | tf_op jit(solution)/shard_map/scale_rows/pallas_call | solution.py:518
